TPU v7x, 128 devices: a whole 4x4x4 slice. The times are simulated.
128 devices in a mesh: blk: 16 (over y, z_lo, core), cross: 8 (over z_hi, x).
Axes of the slice: x: 4, y: 4, z: 4 (z_hi: 2, z_lo: 2; z = z_hi * 2 + z_lo), core: 2. Of those that a mesh axis runs over, the one named last changes fastest.
Arguments:
- receiver_spectra: float32 [16384, 2, 1024], P(('blk', 'cross')), may hold values from -400 to 400
- source_spectra: float32 [16384, 2, 1024], P(('blk', 'cross')), may hold values from -400 to 400
- quality: int32 [16384], P(('blk', 'cross')), may hold values 0 or 1
- slot_order: int32 [128, 128], P(('blk', 'cross')), may hold values from 0 to 127, each once within a row
- owners: int32 [2, 16], replicated, may hold values from 0 to 7
Outputs:
- correlations: bfloat16 [2, 16, 8, 128, 128, 256], P(None, 'blk', 'cross')
Inputs may be any that keep to these rules, and one draw needn't show every extreme that they name: `slot_order`: each row is a permutation of 0 to 127.
All inputs are finite; a program needn't handle non-finite values. No bound on the sum of `quality` on one device may be relied on, other than what follows from the above.
Results may differ from a plain program's by a relative error of at most 0.0056.
Values sent between devices are 32-bit elements; how exact they have to be, the bound alone decides.
No kernel may reach another device: no remote copies, remote signals or barrier semaphores. Data moves between devices by JAX's collectives and lax.ppermute only.
A program may use at most 128 MiB of HBM per device.

v0:
```python
import math

import jax
import jax.numpy as jnp
from jax import lax
from jax.sharding import PartitionSpec as P

L = 256
STEPS = 2


def passed_along(value, axis, steps):
    count = lax.axis_size(axis)
    pairs = [(source, (source + steps) % count) for source in range(count)]
    return lax.ppermute(value, axis, pairs)


def spread(block, axis, holder):
    block = jnp.where(lax.axis_index(axis) == holder, block, jnp.zeros_like(block))
    return lax.psum(block, axis)


def lag_tables(bins, lags):
    bin_index = jnp.arange(bins, dtype=jnp.int32)
    odd_index = 2 * jnp.arange(lags // 2, dtype=jnp.int32) + 1
    phase_turns = jnp.mod(bin_index[:, None] * odd_index[None, :], 4 * bins).astype(jnp.float32)
    phase_angle = phase_turns * (math.pi / (2 * bins))
    cos_table = (jnp.cos(phase_angle) / bins).astype(jnp.bfloat16)
    sin_table = (-jnp.sin(phase_angle) / bins).astype(jnp.bfloat16)
    return (cos_table, sin_table)


def whiten(spectra):
    mean_power = jnp.mean(spectra * spectra, axis=(1, 2), keepdims=True)
    return spectra * lax.rsqrt(mean_power + 1e-06)


def correlate(panel_spec, slab_spec, cos_table, sin_table):
    npanel = panel_spec.shape[0]
    nslab = slab_spec.shape[0]
    width = math.gcd(npanel, 16)
    blocks = panel_spec.reshape(npanel // width, width, 2, panel_spec.shape[2])

    def one_block(source):
        inphase = (
            source[:, None, 0, :] * slab_spec[None, :, 0, :]
            + source[:, None, 1, :] * slab_spec[None, :, 1, :]
        )
        quadrature = (
            source[:, None, 1, :] * slab_spec[None, :, 0, :]
            - source[:, None, 0, :] * slab_spec[None, :, 1, :]
        )
        inphase = inphase.astype(jnp.bfloat16).reshape(width * nslab, -1)
        quadrature = quadrature.astype(jnp.bfloat16).reshape(width * nslab, -1)
        even = jnp.dot(inphase, cos_table, preferred_element_type=jnp.float32)
        odd = jnp.dot(quadrature, sin_table, preferred_element_type=jnp.float32)
        joined = jnp.concatenate([even + odd, even - odd], axis=-1).astype(jnp.bfloat16)
        return joined.reshape(width, nslab, -1)

    lagged = lax.map(one_block, blocks)
    return lagged.reshape(npanel, nslab, lagged.shape[-1])


def local(receiver_spectra, source_spectra, quality, slot_order, owners):
    bins = receiver_spectra.shape[2]
    cos_table, sin_table = lag_tables(bins, L)
    kept = quality.astype(jnp.float32)[:, None, None]
    receivers = whiten(receiver_spectra) * kept
    receivers = jnp.take(receivers, slot_order[0], axis=0)
    sources = whiten(source_spectra)
    block_index = lax.axis_index("blk")
    my_owners = lax.dynamic_index_in_dim(owners, block_index, 1, keepdims=False)
    moving = receivers
    results = []
    for loop_step in range(STEPS):
        if loop_step > 0:
            moving = passed_along(moving, "blk", 1)
        owner_index = my_owners[loop_step]
        panel_spec = spread(sources, "cross", owner_index)
        results.append(correlate(panel_spec, moving, cos_table, sin_table))
    return jnp.stack(results)[:, None, None]


def solution(mesh):
    placed = (
        P(("blk", "cross"), None, None),
        P(("blk", "cross"), None, None),
        P(("blk", "cross")),
        P(("blk", "cross"), None),
        P(),
    )
    return jax.shard_map(
        local,
        mesh=mesh,
        in_specs=placed,
        out_specs=P(None, "blk", "cross", None, None, None),
        check_vma=False,
    )
```

profile of v0, /device:TPU:1, one launch (start us, length us, event | category | flops | bytes accessed | tf_op | source)
XLA Modules:
  0.0 325.4 jit_solution(18305482132003351451)
XLA Ops:
  11.4 3.3 %broadcast_select_fusion.2 = (f32[128,2,1024]{2,1,0:T(2,128)}, f32[128,2,1024]{2,1,0:T(2,128)}) fusion(pred[]{:T(512)S(6)} %eq.8, f32[128,2,1024]{2,1,0:T(2,128)} %param.10, f32[128]{0:T(128)S(1)} %add_rsqrt_fusion.1, pred[]{:T(512)S(6)} %eq.9), kind=kLoop, calls=%fused_computation.81 | loop fusion | flops 786432 | bytes 3146242 | tf_op jit(solution)/shard_map/jit(_where)/select_n | solution.py:19
  22.3 3.3 %collective-permute-start = (f32[128,2,1024]{2,1,0:T(2,128)S(1)}, f32[128,2,1024]{2,1,0:T(2,128)S(1)}, u32[]{:S(2)}, u32[]{:S(2)}) collective-permute-start(f32[128,2,1024]{2,1,0:T(2,128)S(1)} %broadcast_select_fusion), channel_id=1, source_target_pairs={{0,8},{8,16},{16,24},{24,32},{32,40},{40,48},{48,56},{56,64},{64,7... | collective-permute-start | bytes 3145736 | tf_op jit(solution)/shard_map/ppermute | solution.py:15
  25.6 24.8 %collective-permute-done = f32[128,2,1024]{2,1,0:T(2,128)S(1)} collective-permute-done((f32[128,2,1024]{2,1,0:T(2,128)S(1)}, f32[128,2,1024]{2,1,0:T(2,128)S(1)}, u32[]{:S(2)}, u32[]{:S(2)}) %collective-permute-start) | collective-permute-done | bytes 1048608 | tf_op jit(solution)/shard_map/ppermute | solution.py:15
  50.4 60.3 %all-reduce.3.cloned.1.call-done = (f32[8,16,2,1024]{3,2,1,0:T(2,128)}, f32[8,16,2,1024]{3,2,1,0:T(2,128)}) async-done(((f32[8,16,2,1024]{3,2,1,0:T(2,128)}, f32[8,16,2,1024]{3,2,1,0:T(2,128)}), (f32[8,16,2,1024]{3,2,1,0:T(2,128)}, f32[8,16,2,1024]{3,2,1,0:T(2,128)})) %all-reduce.3.cloned.1.call-update) | async-done | bytes 2097168 | tf_op jit(solution)/shard_map/psum | solution.py:20
  110.7 4.3 %broadcast.94.clone = bf16[8,16,128,256]{3,2,1,0:T(8,128)(2,1)} broadcast(bf16[]{:T(256)} %constant.65.clone.1), dimensions={} | broadcast | bytes 8388610 | tf_op jit(solution)/shard_map/broadcast.7
  115.0 92.7 %while.25 = (s32[]{:T(128)}, bf16[8,16,128,256]{3,2,1,0:T(8,128)(2,1)}, f32[8,16,2,1024]{3,2,1,0:T(2,128)}, f32[128,2,1024]{2,1,0:T(2,128)S(1)}, s32[128]{0:T(128)S(1)}, /*index=5*/s32[]{:T(128)}) while((s32[]{:T(128)}, bf16[8,16,128,256]{3,2,1,0:T(8,128)(2,1)}, f32[8,16,2,1024]{3,2,1,0:T(2,128)}, ...), condition=%wide.region_7.8_spmd.clone.clone, body=%wide.region_6.7_spmd.clone.clone.sunk | while | flops 1097990144 | bytes 28181588 | solution.py:60
  119.7 2.9 fusion.81
  131.3 2.9 fusion.81
  134.2 2.8 add_convert_fusion.7
  142.9 2.9 fusion.81
  154.4 2.9 fusion.81
  157.3 2.8 add_convert_fusion.7
  166.0 2.9 fusion.81
  177.6 2.9 fusion.81
  180.5 2.8 add_convert_fusion.7
  189.2 2.9 fusion.81
  192.1 2.8 add_convert_fusion.7
  200.8 2.9 fusion.81
  207.7 4.3 %broadcast.94.clone.1 = bf16[8,16,128,256]{3,2,1,0:T(8,128)(2,1)} broadcast(bf16[]{:T(256)} %constant.65.clone.1), dimensions={} | broadcast | bytes 8388610 | tf_op jit(solution)/shard_map/broadcast.7
  212.0 92.7 %while.24 = (s32[]{:T(128)}, bf16[8,16,128,256]{3,2,1,0:T(8,128)(2,1)}, f32[8,16,2,1024]{3,2,1,0:T(2,128)}, f32[128,2,1024]{2,1,0:T(2,128)S(1)}, s32[128]{0:T(128)S(1)}, /*index=5*/s32[]{:T(128)}) while((s32[]{:T(128)}, bf16[8,16,128,256]{3,2,1,0:T(8,128)(2,1)}, f32[8,16,2,1024]{3,2,1,0:T(2,128)}, ...), condition=%wide.region_4.5_spmd.clone.clone, body=%wide.region_3.4_spmd.clone.clone.sunk | while | flops 1097990144 | bytes 28181588 | solution.py:60
  216.7 2.9 fusion.76
  219.6 2.8 add_convert_fusion.6
  228.4 2.9 fusion.76
  231.3 2.8 add_convert_fusion.6
  240.0 2.9 fusion.76
  251.5 2.9 fusion.76
  254.4 2.8 add_convert_fusion.6
  263.1 2.9 fusion.76
  274.8 2.9 fusion.76
  286.3 2.9 fusion.76
  297.9 2.9 fusion.76
  304.7 13.8 %maximum_bitcast_fusion = bf16[2,1,1,128,128,256]{5,4,3,2,1,0:T(8,128)(2,1)} fusion(bf16[1,128,128,256]{3,2,1,0:T(8,128)(2,1)} %bitcast.87, bf16[1,128,128,256]{3,2,1,0:T(8,128)(2,1)} %bitcast.86), kind=kLoop, calls=%fused_computation.75 | loop fusion | flops 8388608 | bytes 33554432 | tf_op jit(solution)/shard_map/broadcast_in_dim | solution.py:81
  (143 shorter events, 130.3 us)
Async XLA Ops:
  6.5 0.7 copy-start
  6.5 15.2 %copy-start.2 = (s32[1,128]{1,0:T(1,128)S(1)}, s32[1,128]{1,0:T(1,128)}, u32[]{:S(2)}) copy-start(s32[1,128]{1,0:T(1,128)} %param.12) | copy-start | bytes 1540
  6.5 104.2 %all-reduce.3.cloned.1.call-start = ((), (), s32[]{:S(2)}) async-start(), calls=%async_computation | async-start | bytes 4194304 | tf_op jit(solution)/shard_map/psum | solution.py:20
  22.3 28.1 %collective-permute-start = (f32[128,2,1024]{2,1,0:T(2,128)S(1)}, f32[128,2,1024]{2,1,0:T(2,128)S(1)}, u32[]{:S(2)}, u32[]{:S(2)}) collective-permute-start(f32[128,2,1024]{2,1,0:T(2,128)S(1)} %broadcast_select_fusion), channel_id=1, source_target_pairs={{0,8},{8,16},{16,24},{24,32},{32,40},{40,48},{48,56},{56,64},{64,7... | collective-permute-start | bytes 3145736 | tf_op jit(solution)/shard_map/ppermute | solution.py:15
  304.7 13.8 %copy-start.1 = (s32[2,16]{1,0:T(2,128)S(1)}, s32[2,16]{1,0:T(2,128)}, u32[]{:S(2)}) copy-start(s32[2,16]{1,0:T(2,128)} %param.13) | copy-start | bytes 388
Sparse Core Ops, SparseCore 0:
  14.9 95.7 all-reduce.2
where the time goes:
time: 330 us; the launch traced here: 325 us
  matrix products  90.8 us (28%)
  other arithmetic  86.3 us (26%)
  waiting for transfers between devices  85.1 us (26%)
  local copies, waits for them, and re-layouts  44.4 us (13%)
  between operations  14.7 us (4%)
    psum x1, waiting for transfers between devices, spread(): return lax.psum(block, axis)  60.3 us
    dot_general x16, matrix products, one_block(): odd = jnp.dot(quadrature, sin_table, preferred_element_type=jnp.float32)  45.8 us
    dot_general x16, matrix products, one_block(): even = jnp.dot(inphase, cos_table, preferred_element_type=jnp.float32)  45 us
    convert_element_type x16, other arithmetic, one_block(): quadrature = quadrature.astype(jnp.bfloat16).reshape(width * nslab, -1)  42.7 us
    ppermute x1, waiting for transfers between devices, passed_along(): return lax.ppermute(value, axis, pairs)  24.8 us
    dynamic_update_slice x16, other arithmetic, correlate(): lagged = lax.map(one_block, blocks)  18.4 us
    squeeze x16, local copies, waits for them, and re-layouts, correlate(): lagged = lax.map(one_block, blocks)  14.6 us
    broadcast_in_dim x1, other arithmetic, local(): return jnp.stack(results)[:, None, None]  13.8 us
  transfers between devices with their start and end apart: 2, of which 2 were waited for; matrix products, arithmetic and copies ran while one was open for 2% of the time, Pallas kernels for 0%

commit v1 on v0

v1 whole, which is shorter than its diff:
```python
import functools
import math

import jax
import jax.numpy as jnp
from jax import lax
from jax.experimental import pallas as pl
from jax.experimental.pallas import tpu as pltpu
from jax.sharding import PartitionSpec as P

L = 256
STEPS = 2
F32 = jnp.float32
BF16 = jnp.bfloat16
VMEM = pl.BlockSpec(memory_space=pltpu.VMEM)
VMEM_BYTES = 56 << 20


def passed_along(value, axis, steps):
    count = lax.axis_size(axis)
    pairs = [(source, (source + steps) % count) for source in range(count)]
    return lax.ppermute(value, axis, pairs)


def lag_tables(bins, lags):
    bin_index = jnp.arange(bins, dtype=jnp.int32)
    odd_index = 2 * jnp.arange(lags // 2, dtype=jnp.int32) + 1
    phase_turns = jnp.mod(bin_index[:, None] * odd_index[None, :], 4 * bins).astype(F32)
    phase_angle = phase_turns * (math.pi / (2 * bins))
    cos_table = (jnp.cos(phase_angle) / bins).astype(BF16)
    sin_table = (-jnp.sin(phase_angle) / bins).astype(BF16)
    return (cos_table, sin_table)


def prepare_kernel(order_ref, quality_ref, raw_ref, out_ref):
    slots, _, bins = raw_ref.shape

    def eight(step, _):
        base = pl.multiple_of(step * 8, 8)
        real, imag, kept = [], [], []
        for i in range(8):
            channel = order_ref[0, base + i]
            pair = raw_ref[channel]
            real.append(pair[0:1, :])
            imag.append(pair[1:2, :])
            kept.append(jnp.full((1, 1), quality_ref[channel].astype(F32), F32))
        real = jnp.concatenate(real, axis=0)
        imag = jnp.concatenate(imag, axis=0)
        kept = jnp.concatenate(kept, axis=0)
        power = jnp.sum(real * real + imag * imag, axis=1, keepdims=True) / (2 * bins)
        scale = lax.rsqrt(power + 1e-06)
        out_ref[0, pl.ds(base, 8), :] = real * scale * kept
        out_ref[1, pl.ds(base, 8), :] = imag * scale * kept
        return 0

    lax.fori_loop(0, slots // 8, eight, 0)


def prepare(raw, quality, slot_order):
    slots, _, bins = raw.shape
    return pl.pallas_call(
        prepare_kernel,
        out_shape=jax.ShapeDtypeStruct((2, slots, bins), F32),
        in_specs=[
            pl.BlockSpec(memory_space=pltpu.SMEM),
            pl.BlockSpec(memory_space=pltpu.SMEM),
            VMEM,
        ],
        out_specs=VMEM,
        name="prepare",
        cost_estimate=pl.CostEstimate(flops=5 * raw.size, bytes_accessed=8 * raw.size, transcendentals=0),
    )(slot_order, quality, raw)


def correlate_kernel(count, aliased, place_ref, *refs):
    chunks, (slab_ref, cos_ref, sin_ref) = refs[:count], refs[count : count + 3]
    out_ref, white_ref = refs[count + 3 + aliased :]
    width, _, bins = chunks[0].shape
    slots = slab_ref.shape[1]
    half = cos_ref.shape[1]
    step = pl.program_id(0)
    for i in range(count):

        @pl.when(step == i)
        def _():
            raw = chunks[i][...]
            power = jnp.sum(jnp.sum(raw * raw, axis=2, keepdims=True), axis=1, keepdims=True) / (2 * bins)
            white_ref[...] = raw * lax.rsqrt(power + 1e-06)

    slab_re, slab_im = slab_ref[0], slab_ref[1]
    inphase, quadrature = [], []
    for p in range(width):
        pair = white_ref[p]
        re, im = pair[0:1, :], pair[1:2, :]
        inphase.append((re * slab_re + im * slab_im).astype(BF16))
        quadrature.append((im * slab_re - re * slab_im).astype(BF16))
    inphase = jnp.concatenate(inphase, axis=0)
    quadrature = jnp.concatenate(quadrature, axis=0)
    even = jnp.dot(inphase, cos_ref[...], preferred_element_type=F32)
    odd = jnp.dot(quadrature, sin_ref[...], preferred_element_type=F32)
    for p in range(width):
        e = even[p * slots : (p + 1) * slots]
        o = odd[p * slots : (p + 1) * slots]
        out_ref[p, :, :half] = (e + o).astype(BF16)
        out_ref[p, :, half:] = (e - o).astype(BF16)


def correlate(out, step, chunks, places, slab, cos_table, sin_table, sources):
    count = len(chunks)
    width, _, bins = chunks[0].shape
    slots = slab.shape[1]
    half = cos_table.shape[1]
    aliased = out is not None
    args = [*chunks, slab, cos_table, sin_table] + ([out] if aliased else [])
    grid_spec = pltpu.PrefetchScalarGridSpec(
        num_scalar_prefetch=1,
        grid=(count,),
        in_specs=[VMEM] * (count + 3) + ([pl.BlockSpec(memory_space=pl.ANY)] if aliased else []),
        out_specs=pl.BlockSpec((None, width, slots, 2 * half), lambda i, place: (step, place[i], 0, 0)),
        scratch_shapes=[pltpu.VMEM((width, 2, bins), F32)],
    )
    return pl.pallas_call(
        functools.partial(correlate_kernel, count, aliased),
        out_shape=jax.ShapeDtypeStruct((STEPS, sources, slots, 2 * half), BF16),
        grid_spec=grid_spec,
        input_output_aliases={count + 4: 0} if aliased else {},
        compiler_params=pltpu.CompilerParams(vmem_limit_bytes=VMEM_BYTES),
        name="correlate",
        cost_estimate=pl.CostEstimate(
            flops=count * width * slots * bins * 4 * 2 * half,
            bytes_accessed=count * width * slots * 2 * half * 2 + 8 * slots * bins,
            transcendentals=0,
        ),
    )(jnp.stack(places).astype(jnp.int32), *args)


def local(receiver_spectra, source_spectra, quality, slot_order, owners):
    sources, _, bins = source_spectra.shape
    members = lax.axis_size("cross")
    width = sources // members
    cos_table, sin_table = lag_tables(bins, L)
    me = lax.axis_index("cross")
    my_owners = lax.dynamic_index_in_dim(owners, lax.axis_index("blk"), 1, keepdims=False)

    slab0 = prepare(receiver_spectra, quality, slot_order)
    slab1 = passed_along(slab0, "blk", 1)
    slabs = [slab0, slab1]

    shares = lax.all_to_all(source_spectra.reshape(members, width, 2, bins), "cross", 0, 0)
    own = [lax.dynamic_index_in_dim(shares, my_owners[s], 0, keepdims=False) for s in range(STEPS)]
    chunks = [[own[s]] + [passed_along(own[s], "cross", d) for d in range(1, members)] for s in range(STEPS)]
    places = [(me - d) % members for d in range(members)]

    out = None
    for s, group in [(0, [0]), (0, [1, 2, 3]), (0, [4, 5, 6, 7]), (1, [0, 1, 2, 3, 4, 5, 6, 7])]:
        out = correlate(
            out, s, [chunks[s][d] for d in group], [places[d] for d in group],
            slabs[s], cos_table, sin_table, sources,
        )
    return out[:, None, None]


def solution(mesh):
    placed = (
        P(("blk", "cross"), None, None),
        P(("blk", "cross"), None, None),
        P(("blk", "cross")),
        P(("blk", "cross"), None),
        P(),
    )
    return jax.shard_map(
        local,
        mesh=mesh,
        in_specs=placed,
        out_specs=P(None, "blk", "cross", None, None, None),
        check_vma=False,
    )
```

time: 330 us -> 131 us (0.40)
  the two profiles are of different devices: /device:TPU:1 before, /device:TPU:40 now
where the time goes in v1:
time: 131 us; the launch traced here: 130 us
  Pallas kernels  66.4 us (51%)
  starting transfers between devices  42.8 us (33%)
  waiting for transfers between devices  9.92 us (8%)
  other arithmetic  4.22 us (3%)
  between operations  3.92 us (3%)
  local copies, waits for them, and re-layouts  2.97 us (2%)
    pallas_call x4, Pallas kernels, correlate(): pl.pallas_call(functools.partial(correlate_kernel, count, aliased), out_s...  62.2 us
    ppermute x15, starting transfers between devices, passed_along(): return lax.ppermute(value, axis, pairs)  35.9 us
    all_to_all x1, waiting for transfers between devices, local(): lax.all_to_all(source_spectra.reshape(members, width, 2, bins), 'cross',...  9.88 us
    all_to_all x1, starting transfers between devices, local(): lax.all_to_all(source_spectra.reshape(members, width, 2, bins), 'cross',...  6.85 us
    pallas_call x1, Pallas kernels, prepare(): pl.pallas_call(prepare_kernel, out_shape=jax.ShapeDtypeStruct((2, slots,...  4.2 us
    convert_element_type x1, other arithmetic, lag_tables(): sin_table = (-jnp.sin(phase_angle) / bins).astype(BF16)  3.02 us
  transfers between devices with their start and end apart: 16, of which 1 were waited for; matrix products, arithmetic and copies ran while one was open for 4% of the time, Pallas kernels for 29%

profile of v1, /device:TPU:40, one launch (start us, length us, event | category | flops | bytes accessed | tf_op | source)
XLA Modules:
  0.0 130.3 jit_solution(4598027409922472918)
XLA Ops:
  0.0 6.8 %all-to-all-start = ((f32[8,16,2,1024]{3,2,1,0:T(2,128)}), f32[8,16,2,1024]{3,2,1,0:T(2,128)S(1)}, u32[]{:S(2)}, u32[]{:S(2)}) async-start(f32[8,16,2,1024]{3,2,1,0:T(2,128)} %bitcast.18), calls=%async_computation | async-start | bytes 2097152 | tf_op jit(solution)/shard_map/all_to_all | solution.py:149
  6.9 0.1 constant_dynamic-slice_fusion
  6.9 0.5 fusion.6
  11.2 3.0 %multiply_convert_fusion = (bf16[1024,128]{1,0:T(8,128)(2,1)}, bf16[1024,128]{1,0:T(8,128)(2,1)}) fusion(s32[128]{0:T(128)S(1)} %multiply_add_fusion), kind=kLoop, calls=%fused_computation.6 | loop fusion | flops 2490368 | bytes 524800 | tf_op jit(solution)/shard_map/convert_element_type | solution.py:31
  14.2 9.9 %all-to-all-done = f32[8,16,2,1024]{3,2,1,0:T(2,128)S(1)} async-done(((f32[8,16,2,1024]{3,2,1,0:T(2,128)}), f32[8,16,2,1024]{3,2,1,0:T(2,128)S(1)}, u32[]{:S(2)}, u32[]{:S(2)}) %all-to-all-start) | async-done | bytes 1048608 | tf_op jit(solution)/shard_map/all_to_all | solution.py:149
  24.1 0.9 collective-permute-start.12
  25.0 0.6 pad_add_fusion.1.place_ref
  25.6 0.6 stack.49.place_ref
  26.2 4.2 %prepare.1.refs_1_.refs_3_.refs_4_ = f32[2,128,1024]{2,1,0:T(8,128)} custom-call(s32[1,128]{1,0:T(1,128)} %order_ref.1, s32[128]{0:T(128)} %quality_ref.1, f32[128,2,1024]{2,1,0:T(2,128)} %raw_ref.1), custom_call_target="tpu_custom_call" | custom-call | flops 1310720 | bytes 2097152 | tf_op jit(solution)/shard_map/prepare/pallas_call | solution.py:61
  30.4 0.6 pad_add_fusion.place_ref
  31.0 1.2 collective-permute-start.13
  32.2 1.5 %collective-permute-start.14 = (f32[16,2,1024]{2,1,0:T(2,128)S(1)}, f32[16,2,1024]{2,1,0:T(2,128)S(1)}, u32[]{:S(2)}, u32[]{:S(2)}) collective-permute-start(f32[16,2,1024]{2,1,0:T(2,128)S(1)} %get-tuple-element.5.refs_0_), channel_id=1, source_target_pairs={{0,3},{1,4},{2,5},{3,6},{4,7},{5,0},{6,1},{7,2},{8,11},{9,12},{10,... | collective-permute-start | bytes 393224 | tf_op jit(solution)/shard_map/ppermute | solution.py:22
  33.7 5.0 %collective-permute-start.10 = (f32[16,2,1024]{2,1,0:T(2,128)S(1)}, f32[16,2,1024]{2,1,0:T(2,128)S(1)}, u32[]{:S(2)}, u32[]{:S(2)}) collective-permute-start(f32[16,2,1024]{2,1,0:T(2,128)S(1)} %get-tuple-element.5.refs_0_), channel_id=1, source_target_pairs={{0,6},{1,7},{2,0},{3,1},{4,2},{5,3},{6,4},{7,5},{8,14},{9,15},{10,... | collective-permute-start | bytes 393224 | tf_op jit(solution)/shard_map/ppermute | solution.py:22
  38.7 0.6 collective-permute-start.11
  39.4 2.4 %collective-permute-start.8 = (f32[16,2,1024]{2,1,0:T(2,128)S(1)}, f32[16,2,1024]{2,1,0:T(2,128)S(1)}, u32[]{:S(2)}, u32[]{:S(2)}) collective-permute-start(f32[16,2,1024]{2,1,0:T(2,128)S(1)} %get-tuple-element.5.refs_0_), channel_id=1, source_target_pairs={{0,4},{1,5},{2,6},{3,7},{4,0},{5,1},{6,2},{7,3},{8,12},{9,13},{10,... | collective-permute-start | bytes 393224 | tf_op jit(solution)/shard_map/ppermute | solution.py:22
  41.8 5.1 %correlate.4.refs_6_ = bf16[2,128,128,256]{3,2,1,0:T(8,128)(2,1)} custom-call(s32[1]{0:T(128)} %bitcast.place_ref, f32[16,2,1024]{2,1,0:T(2,128)} %copy-done.2, f32[2,128,1024]{2,1,0:T(8,128)} %prepare.1.refs_1_.refs_3_.refs_4_, bf16[1024,128]{1,0:T(8,128)(2,1)} %get-tuple-element.10.refs_2_.refs_4_.refs_5_.refs_9_, ...), custom_call_target="tpu_custom_call" | custom-call | flops 2147483648 | bytes 2097152 | tf_op jit(solution)/shard_map/correlate/pallas_call | solution.py:122
  46.9 0.1 collective-permute-start.7
  47.0 2.0 %collective-permute-start.9 = (f32[16,2,1024]{2,1,0:T(2,128)}, f32[16,2,1024]{2,1,0:T(2,128)S(1)}, u32[]{:S(2)}, u32[]{:S(2)}) collective-permute-start(f32[16,2,1024]{2,1,0:T(2,128)} %copy-done.2), channel_id=1, source_target_pairs={{0,5},{1,6},{2,7},{3,0},{4,1},{5,2},{6,3},{7,4},{8,13},{9,14},{10,... | collective-permute-start | bytes 393224 | tf_op jit(solution)/shard_map/ppermute | solution.py:22
  49.0 0.1 collective-permute-start
  49.1 2.7 %collective-permute-start.1 = (f32[16,2,1024]{2,1,0:T(2,128)S(1)}, f32[16,2,1024]{2,1,0:T(2,128)S(1)}, u32[]{:S(2)}, u32[]{:S(2)}) collective-permute-start(f32[16,2,1024]{2,1,0:T(2,128)S(1)} %get-tuple-element.6.refs_0_), channel_id=1, source_target_pairs={{0,2},{1,3},{2,4},{3,5},{4,6},{5,7},{6,0},{7,1},{8,10},{9,11},{10,... | collective-permute-start | bytes 393224 | tf_op jit(solution)/shard_map/ppermute | solution.py:22
  51.8 13.1 %collective-permute-start.2 = (f32[16,2,1024]{2,1,0:T(2,128)S(1)}, f32[16,2,1024]{2,1,0:T(2,128)S(1)}, u32[]{:S(2)}, u32[]{:S(2)}) collective-permute-start(f32[16,2,1024]{2,1,0:T(2,128)S(1)} %get-tuple-element.6.refs_0_), channel_id=1, source_target_pairs={{0,3},{1,4},{2,5},{3,6},{4,7},{5,0},{6,1},{7,2},{8,11},{9,12},{10,... | collective-permute-start | bytes 393224 | tf_op jit(solution)/shard_map/ppermute | solution.py:22
  64.9 12.6 %correlate.5.refs_7_ = bf16[2,128,128,256]{3,2,1,0:T(8,128)(2,1)} custom-call(s32[3]{0:T(128)} %pad_add_fusion.1.place_ref, f32[16,2,1024]{2,1,0:T(2,128)} %copy-done.3, f32[16,2,1024]{2,1,0:T(2,128)} %copy-done.8, f32[16,2,1024]{2,1,0:T(2,128)} %copy-done.9, f32[2,128,1024]{2,1,0:T(8,128)} %prepare.1.refs_1_.refs_3_.refs_4_, ...), custom_call_target="tpu_custom_call", output_to_operand_aliasing={{}: (7, {})} | custom-call | flops 6442450944 | bytes 4194304 | tf_op jit(solution)/shard_map/correlate/pallas_call | solution.py:122
  77.5 0.1 collective-permute-start.3
  77.6 0.3 collective-permute-start.4
  77.9 3.9 %collective-permute-start.5 = (f32[16,2,1024]{2,1,0:T(2,128)S(1)}, f32[16,2,1024]{2,1,0:T(2,128)S(1)}, u32[]{:S(2)}, u32[]{:S(2)}) collective-permute-start(f32[16,2,1024]{2,1,0:T(2,128)S(1)} %get-tuple-element.6.refs_0_), channel_id=1, source_target_pairs={{0,6},{1,7},{2,0},{3,1},{4,2},{5,3},{6,4},{7,5},{8,14},{9,15},{10,... | collective-permute-start | bytes 393224 | tf_op jit(solution)/shard_map/ppermute | solution.py:22
  81.8 2.1 %collective-permute-start.6 = (f32[16,2,1024]{2,1,0:T(2,128)S(1)}, f32[16,2,1024]{2,1,0:T(2,128)S(1)}, u32[]{:S(2)}, u32[]{:S(2)}) collective-permute-start(f32[16,2,1024]{2,1,0:T(2,128)S(1)} %get-tuple-element.6.refs_0_), channel_id=1, source_target_pairs={{0,7},{1,0},{2,1},{3,2},{4,3},{5,4},{6,5},{7,6},{8,15},{9,8},{10,9... | collective-permute-start | bytes 393224 | tf_op jit(solution)/shard_map/ppermute | solution.py:22
  83.9 15.8 %correlate.6.refs_11_ = bf16[2,128,128,256]{3,2,1,0:T(8,128)(2,1)} custom-call(s32[4]{0:T(128)} %pad_add_fusion.place_ref, f32[16,2,1024]{2,1,0:T(2,128)} %copy-done.6, f32[16,2,1024]{2,1,0:T(2,128)} %copy-done.7, f32[16,2,1024]{2,1,0:T(2,128)} %copy-done.4, f32[16,2,1024]{2,1,0:T(2,128)} %copy-done.5, ...), custom_call_target="tpu_custom_call", output_to_operand_aliasing={{}: (8, {})} | custom-call | flops 8589934592 | bytes 5242880 | tf_op jit(solution)/shard_map/correlate/pallas_call | solution.py:122
  99.8 0.6 copy-done.15
  100.4 0.1 copy-done.17
  100.5 0.0 copy-done.18
  100.5 1.0 copy-done.11
  101.5 28.8 %correlate.7 = bf16[2,128,128,256]{3,2,1,0:T(8,128)(2,1)} custom-call(s32[8]{0:T(128)} %stack.49.place_ref, f32[16,2,1024]{2,1,0:T(2,128)} %copy-done.10, f32[16,2,1024]{2,1,0:T(2,128)} %copy-done.12, f32[16,2,1024]{2,1,0:T(2,128)} %copy-done.13, f32[16,2,1024]{2,1,0:T(2,128)} %copy-done.14, ...), custom_call_target="tpu_custom_call", output_to_operand_aliasing={{}: (12, {})} | custom-call | flops 17179869184 | bytes 9437184 | tf_op jit(solution)/shard_map/correlate/pallas_call | solution.py:122
  (51 shorter events, 0.2 us)
Async XLA Ops:
  0.0 6.9 %copy-start = (s32[2,16]{1,0:T(2,128)S(1)}, s32[2,16]{1,0:T(2,128)}, u32[]{:S(2)}) copy-start(s32[2,16]{1,0:T(2,128)} %param.9) | copy-start | bytes 388
  0.0 24.1 %all-to-all-start = ((f32[8,16,2,1024]{3,2,1,0:T(2,128)}), f32[8,16,2,1024]{3,2,1,0:T(2,128)S(1)}, u32[]{:S(2)}, u32[]{:S(2)}) async-start(f32[8,16,2,1024]{3,2,1,0:T(2,128)} %bitcast.18), calls=%async_computation | async-start | bytes 2097152 | tf_op jit(solution)/shard_map/all_to_all | solution.py:149
  24.1 17.7 %copy-start.2 = (f32[16,2,1024]{2,1,0:T(2,128)}, f32[16,2,1024]{2,1,0:T(2,128)S(1)}, u32[]{:S(2)}) copy-start(f32[16,2,1024]{2,1,0:T(2,128)S(1)} %get-tuple-element.5.refs_0_) | copy-start | bytes 393220
  24.1 57.7 %copy-start.10 = (f32[16,2,1024]{2,1,0:T(2,128)}, f32[16,2,1024]{2,1,0:T(2,128)S(1)}, u32[]{:S(2)}) copy-start(f32[16,2,1024]{2,1,0:T(2,128)S(1)} %get-tuple-element.6.refs_0_) | copy-start | bytes 393220
  24.1 15.3 %collective-permute-start.12 = (f32[16,2,1024]{2,1,0:T(2,128)S(1)}, f32[16,2,1024]{2,1,0:T(2,128)S(1)}, u32[]{:S(2)}, u32[]{:S(2)}) collective-permute-start(f32[16,2,1024]{2,1,0:T(2,128)S(1)} %get-tuple-element.5.refs_0_), channel_id=1, source_target_pairs={{0,1},{1,2},{2,3},{3,4},{4,5},{5,6},{6,7},{7,0},{8,9},{9,10},{10,1... | collective-permute-start | bytes 393224 | tf_op jit(solution)/shard_map/ppermute | solution.py:22
  30.4 16.5 %copy-start.1 = (f32[2,128,1024]{2,1,0:T(8,128)S(1)}, f32[2,128,1024]{2,1,0:T(8,128)}, u32[]{:S(2)}) copy-start(f32[2,128,1024]{2,1,0:T(8,128)} %prepare.1.refs_1_.refs_3_.refs_4_) | copy-start | bytes 3145732
  31.0 15.9 %collective-permute-start.13 = (f32[16,2,1024]{2,1,0:T(2,128)S(1)}, f32[16,2,1024]{2,1,0:T(2,128)S(1)}, u32[]{:S(2)}, u32[]{:S(2)}) collective-permute-start(f32[16,2,1024]{2,1,0:T(2,128)S(1)} %get-tuple-element.5.refs_0_), channel_id=1, source_target_pairs={{0,2},{1,3},{2,4},{3,5},{4,6},{5,7},{6,0},{7,1},{8,10},{9,11},{10,... | collective-permute-start | bytes 393224 | tf_op jit(solution)/shard_map/ppermute | solution.py:22
  32.2 14.8 %collective-permute-start.14 = (f32[16,2,1024]{2,1,0:T(2,128)S(1)}, f32[16,2,1024]{2,1,0:T(2,128)S(1)}, u32[]{:S(2)}, u32[]{:S(2)}) collective-permute-start(f32[16,2,1024]{2,1,0:T(2,128)S(1)} %get-tuple-element.5.refs_0_), channel_id=1, source_target_pairs={{0,3},{1,4},{2,5},{3,6},{4,7},{5,0},{6,1},{7,2},{8,11},{9,12},{10,... | collective-permute-start | bytes 393224 | tf_op jit(solution)/shard_map/ppermute | solution.py:22
  33.7 15.3 %collective-permute-start.10 = (f32[16,2,1024]{2,1,0:T(2,128)S(1)}, f32[16,2,1024]{2,1,0:T(2,128)S(1)}, u32[]{:S(2)}, u32[]{:S(2)}) collective-permute-start(f32[16,2,1024]{2,1,0:T(2,128)S(1)} %get-tuple-element.5.refs_0_), channel_id=1, source_target_pairs={{0,6},{1,7},{2,0},{3,1},{4,2},{5,3},{6,4},{7,5},{8,14},{9,15},{10,... | collective-permute-start | bytes 393224 | tf_op jit(solution)/shard_map/ppermute | solution.py:22
  38.7 10.4 %collective-permute-start.11 = (f32[16,2,1024]{2,1,0:T(2,128)S(1)}, f32[16,2,1024]{2,1,0:T(2,128)S(1)}, u32[]{:S(2)}, u32[]{:S(2)}) collective-permute-start(f32[16,2,1024]{2,1,0:T(2,128)S(1)} %get-tuple-element.5.refs_0_), channel_id=1, source_target_pairs={{0,7},{1,0},{2,1},{3,2},{4,3},{5,4},{6,5},{7,6},{8,15},{9,8},{10,9... | collective-permute-start | bytes 393224 | tf_op jit(solution)/shard_map/ppermute | solution.py:22
  39.4 25.5 %copy-start.3 = (f32[16,2,1024]{2,1,0:T(2,128)}, f32[16,2,1024]{2,1,0:T(2,128)S(1)}, u32[]{:S(2)}) copy-start(f32[16,2,1024]{2,1,0:T(2,128)S(1)} %collective-permute-done.12.refs_0_) | copy-start | bytes 393220
  39.4 12.4 %collective-permute-start.8 = (f32[16,2,1024]{2,1,0:T(2,128)S(1)}, f32[16,2,1024]{2,1,0:T(2,128)S(1)}, u32[]{:S(2)}, u32[]{:S(2)}) collective-permute-start(f32[16,2,1024]{2,1,0:T(2,128)S(1)} %get-tuple-element.5.refs_0_), channel_id=1, source_target_pairs={{0,4},{1,5},{2,6},{3,7},{4,0},{5,1},{6,2},{7,3},{8,12},{9,13},{10,... | collective-permute-start | bytes 393224 | tf_op jit(solution)/shard_map/ppermute | solution.py:22
  46.9 18.0 %copy-start.8 = (f32[16,2,1024]{2,1,0:T(2,128)}, f32[16,2,1024]{2,1,0:T(2,128)S(1)}, u32[]{:S(2)}) copy-start(f32[16,2,1024]{2,1,0:T(2,128)S(1)} %collective-permute-done.13.refs_1_) | copy-start | bytes 393220
  46.9 52.9 %collective-permute-start.7 = (f32[2,128,1024]{2,1,0:T(8,128)S(1)}, f32[2,128,1024]{2,1,0:T(8,128)S(1)}, u32[]{:S(2)}, u32[]{:S(2)}) collective-permute-start(f32[2,128,1024]{2,1,0:T(8,128)S(1)} %copy-done.1), channel_id=1, source_target_pairs={{0,8},{8,16},{16,24},{24,32},{32,40},{40,48},{48,56},{56,64},{64,7... | collective-permute-start | bytes 3145736 | tf_op jit(solution)/shard_map/ppermute | solution.py:22
  47.0 17.9 %copy-start.9 = (f32[16,2,1024]{2,1,0:T(2,128)}, f32[16,2,1024]{2,1,0:T(2,128)S(1)}, u32[]{:S(2)}) copy-start(f32[16,2,1024]{2,1,0:T(2,128)S(1)} %collective-permute-done.14.refs_2_) | copy-start | bytes 393220
  47.0 30.5 %collective-permute-start.9 = (f32[16,2,1024]{2,1,0:T(2,128)}, f32[16,2,1024]{2,1,0:T(2,128)S(1)}, u32[]{:S(2)}, u32[]{:S(2)}) collective-permute-start(f32[16,2,1024]{2,1,0:T(2,128)} %copy-done.2), channel_id=1, source_target_pairs={{0,5},{1,6},{2,7},{3,0},{4,1},{5,2},{6,3},{7,4},{8,13},{9,14},{10,... | collective-permute-start | bytes 393224 | tf_op jit(solution)/shard_map/ppermute | solution.py:22
  49.0 28.4 %copy-start.4 = (f32[16,2,1024]{2,1,0:T(2,128)}, f32[16,2,1024]{2,1,0:T(2,128)S(1)}, u32[]{:S(2)}) copy-start(f32[16,2,1024]{2,1,0:T(2,128)S(1)} %collective-permute-done.10.refs_2_) | copy-start | bytes 393220
  49.0 28.5 %collective-permute-start = (f32[16,2,1024]{2,1,0:T(2,128)S(1)}, f32[16,2,1024]{2,1,0:T(2,128)S(1)}, u32[]{:S(2)}, u32[]{:S(2)}) collective-permute-start(f32[16,2,1024]{2,1,0:T(2,128)S(1)} %get-tuple-element.6.refs_0_), channel_id=1, source_target_pairs={{0,1},{1,2},{2,3},{3,4},{4,5},{5,6},{6,7},{7,0},{8,9},{9,10},{10,1... | collective-permute-start | bytes 393224 | tf_op jit(solution)/shard_map/ppermute | solution.py:22
  49.1 28.3 %copy-start.5 = (f32[16,2,1024]{2,1,0:T(2,128)}, f32[16,2,1024]{2,1,0:T(2,128)S(1)}, u32[]{:S(2)}) copy-start(f32[16,2,1024]{2,1,0:T(2,128)S(1)} %collective-permute-done.11.refs_3_) | copy-start | bytes 393220
  49.1 28.7 %collective-permute-start.1 = (f32[16,2,1024]{2,1,0:T(2,128)S(1)}, f32[16,2,1024]{2,1,0:T(2,128)S(1)}, u32[]{:S(2)}, u32[]{:S(2)}) collective-permute-start(f32[16,2,1024]{2,1,0:T(2,128)S(1)} %get-tuple-element.6.refs_0_), channel_id=1, source_target_pairs={{0,2},{1,3},{2,4},{3,5},{4,6},{5,7},{6,0},{7,1},{8,10},{9,11},{10,... | collective-permute-start | bytes 393224 | tf_op jit(solution)/shard_map/ppermute | solution.py:22
  51.8 25.7 %copy-start.6 = (f32[16,2,1024]{2,1,0:T(2,128)}, f32[16,2,1024]{2,1,0:T(2,128)S(1)}, u32[]{:S(2)}) copy-start(f32[16,2,1024]{2,1,0:T(2,128)S(1)} %collective-permute-done.8.refs_0_) | copy-start | bytes 393220
  51.8 29.9 %collective-permute-start.2 = (f32[16,2,1024]{2,1,0:T(2,128)S(1)}, f32[16,2,1024]{2,1,0:T(2,128)S(1)}, u32[]{:S(2)}, u32[]{:S(2)}) collective-permute-start(f32[16,2,1024]{2,1,0:T(2,128)S(1)} %get-tuple-element.6.refs_0_), channel_id=1, source_target_pairs={{0,3},{1,4},{2,5},{3,6},{4,7},{5,0},{6,1},{7,2},{8,11},{9,12},{10,... | collective-permute-start | bytes 393224 | tf_op jit(solution)/shard_map/ppermute | solution.py:22
  77.5 6.4 %copy-start.7 = (f32[16,2,1024]{2,1,0:T(2,128)}, f32[16,2,1024]{2,1,0:T(2,128)S(1)}, u32[]{:S(2)}) copy-start(f32[16,2,1024]{2,1,0:T(2,128)S(1)} %collective-permute-done.9.refs_1_) | copy-start | bytes 393220
  77.5 22.2 %collective-permute-start.3 = (f32[16,2,1024]{2,1,0:T(2,128)S(1)}, f32[16,2,1024]{2,1,0:T(2,128)S(1)}, u32[]{:S(2)}, u32[]{:S(2)}) collective-permute-start(f32[16,2,1024]{2,1,0:T(2,128)S(1)} %get-tuple-element.6.refs_0_), channel_id=1, source_target_pairs={{0,4},{1,5},{2,6},{3,7},{4,0},{5,1},{6,2},{7,3},{8,12},{9,13},{10,... | collective-permute-start | bytes 393224 | tf_op jit(solution)/shard_map/ppermute | solution.py:22
  77.6 22.1 %copy-start.12 = (f32[16,2,1024]{2,1,0:T(2,128)}, f32[16,2,1024]{2,1,0:T(2,128)S(1)}, u32[]{:S(2)}) copy-start(f32[16,2,1024]{2,1,0:T(2,128)S(1)} %collective-permute-done.refs_1_) | copy-start | bytes 393220
  77.6 22.1 %collective-permute-start.4 = (f32[16,2,1024]{2,1,0:T(2,128)S(1)}, f32[16,2,1024]{2,1,0:T(2,128)S(1)}, u32[]{:S(2)}, u32[]{:S(2)}) collective-permute-start(f32[16,2,1024]{2,1,0:T(2,128)S(1)} %get-tuple-element.6.refs_0_), channel_id=1, source_target_pairs={{0,5},{1,6},{2,7},{3,0},{4,1},{5,2},{6,3},{7,4},{8,13},{9,14},{10,... | collective-permute-start | bytes 393224 | tf_op jit(solution)/shard_map/ppermute | solution.py:22
  77.9 21.8 %copy-start.13 = (f32[16,2,1024]{2,1,0:T(2,128)}, f32[16,2,1024]{2,1,0:T(2,128)S(1)}, u32[]{:S(2)}) copy-start(f32[16,2,1024]{2,1,0:T(2,128)S(1)} %collective-permute-done.1.refs_2_) | copy-start | bytes 393220
  77.9 21.9 %collective-permute-start.5 = (f32[16,2,1024]{2,1,0:T(2,128)S(1)}, f32[16,2,1024]{2,1,0:T(2,128)S(1)}, u32[]{:S(2)}, u32[]{:S(2)}) collective-permute-start(f32[16,2,1024]{2,1,0:T(2,128)S(1)} %get-tuple-element.6.refs_0_), channel_id=1, source_target_pairs={{0,6},{1,7},{2,0},{3,1},{4,2},{5,3},{6,4},{7,5},{8,14},{9,15},{10,... | collective-permute-start | bytes 393224 | tf_op jit(solution)/shard_map/ppermute | solution.py:22
  81.8 17.9 %copy-start.14 = (f32[16,2,1024]{2,1,0:T(2,128)}, f32[16,2,1024]{2,1,0:T(2,128)S(1)}, u32[]{:S(2)}) copy-start(f32[16,2,1024]{2,1,0:T(2,128)S(1)} %collective-permute-done.2.refs_3_) | copy-start | bytes 393220
  81.8 18.0 %collective-permute-start.6 = (f32[16,2,1024]{2,1,0:T(2,128)S(1)}, f32[16,2,1024]{2,1,0:T(2,128)S(1)}, u32[]{:S(2)}, u32[]{:S(2)}) collective-permute-start(f32[16,2,1024]{2,1,0:T(2,128)S(1)} %get-tuple-element.6.refs_0_), channel_id=1, source_target_pairs={{0,7},{1,0},{2,1},{3,2},{4,3},{5,4},{6,5},{7,6},{8,15},{9,8},{10,9... | collective-permute-start | bytes 393224 | tf_op jit(solution)/shard_map/ppermute | solution.py:22
  99.8 0.8 copy-start.18
  100.5 1.0 copy-start.11
  (3 other events, 2.1 us)

commit v2 on v1

--- a/solution.py
+++ b/solution.py
@@ -72,25 +72,45 @@
     )(slot_order, quality, raw)
 
 
-def correlate_kernel(count, aliased, place_ref, *refs):
-    chunks, (slab_ref, cos_ref, sin_ref) = refs[:count], refs[count : count + 3]
-    out_ref, white_ref = refs[count + 3 + aliased :]
-    width, _, bins = chunks[0].shape
+def select_kernel(mine_ref, raw_ref, own_ref, copies_ref):
+    raw = raw_ref[...]
+    count = 2 * raw.shape[2]
+    power = jnp.sum(jnp.sum(raw * raw, axis=2, keepdims=True), axis=1, keepdims=True) / count
+    white = raw * lax.rsqrt(power + 1e-06)
+    own_ref[...] = white
+    for i in range(copies_ref.shape[0]):
+        copies_ref[i] = white
+
+
+def select(shares, owner):
+    members = shares.shape[0]
+    share = shares.shape[1:]
+    zeros = (0,) * len(share)
+    return pl.pallas_call(
+        select_kernel,
+        out_shape=(jax.ShapeDtypeStruct(share, F32), jax.ShapeDtypeStruct(shares.shape, F32)),
+        grid_spec=pltpu.PrefetchScalarGridSpec(
+            num_scalar_prefetch=1,
+            grid=(1,),
+            in_specs=[pl.BlockSpec((None,) + share, lambda i, mine: (mine[0],) + zeros)],
+            out_specs=(
+                pl.BlockSpec(share, lambda i, mine: zeros),
+                pl.BlockSpec((members,) + share, lambda i, mine: (0,) + zeros),
+            ),
+        ),
+        name="select",
+    )(owner, shares)
+
+
+def correlate_kernel(aliased, place_ref, panel_ref, slab_ref, cos_ref, sin_ref, *refs):
+    out_ref = refs[aliased]
+    width = panel_ref.shape[0]
     slots = slab_ref.shape[1]
     half = cos_ref.shape[1]
-    step = pl.program_id(0)
-    for i in range(count):
-
-        @pl.when(step == i)
-        def _():
-            raw = chunks[i][...]
-            power = jnp.sum(jnp.sum(raw * raw, axis=2, keepdims=True), axis=1, keepdims=True) / (2 * bins)
-            white_ref[...] = raw * lax.rsqrt(power + 1e-06)
-
     slab_re, slab_im = slab_ref[0], slab_ref[1]
     inphase, quadrature = [], []
     for p in range(width):
-        pair = white_ref[p]
+        pair = panel_ref[p]
         re, im = pair[0:1, :], pair[1:2, :]
         inphase.append((re * slab_re + im * slab_im).astype(BF16))
         quadrature.append((im * slab_re - re * slab_im).astype(BF16))
@@ -105,25 +125,30 @@
         out_ref[p, :, half:] = (e - o).astype(BF16)
 
 
-def correlate(out, step, chunks, places, slab, cos_table, sin_table, sources):
-    count = len(chunks)
-    width, _, bins = chunks[0].shape
+def correlate(out, step, panel, me, slab, tables, sources):
+    width, _, bins = panel.shape[-3:]
     slots = slab.shape[1]
-    half = cos_table.shape[1]
+    half = tables[0].shape[1]
     aliased = out is not None
-    args = [*chunks, slab, cos_table, sin_table] + ([out] if aliased else [])
+    if panel.ndim == 3:
+        count = 1
+        place = lambda i, mine: mine[0]
+        panel_spec = pl.BlockSpec((width, 2, bins), lambda i, mine: (0, 0, 0))
+    else:
+        count = panel.shape[0] - 1
+        place = lambda i, mine: i + (i >= mine[0]).astype(jnp.int32)
+        panel_spec = pl.BlockSpec((None, width, 2, bins), lambda i, mine: (place(i, mine), 0, 0, 0))
     grid_spec = pltpu.PrefetchScalarGridSpec(
         num_scalar_prefetch=1,
         grid=(count,),
-        in_specs=[VMEM] * (count + 3) + ([pl.BlockSpec(memory_space=pl.ANY)] if aliased else []),
-        out_specs=pl.BlockSpec((None, width, slots, 2 * half), lambda i, place: (step, place[i], 0, 0)),
-        scratch_shapes=[pltpu.VMEM((width, 2, bins), F32)],
+        in_specs=[panel_spec, VMEM, VMEM, VMEM] + ([pl.BlockSpec(memory_space=pl.ANY)] if aliased else []),
+        out_specs=pl.BlockSpec((None, width, slots, 2 * half), lambda i, mine: (step, place(i, mine), 0, 0)),
     )
     return pl.pallas_call(
-        functools.partial(correlate_kernel, count, aliased),
+        functools.partial(correlate_kernel, int(aliased)),
         out_shape=jax.ShapeDtypeStruct((STEPS, sources, slots, 2 * half), BF16),
         grid_spec=grid_spec,
-        input_output_aliases={count + 4: 0} if aliased else {},
+        input_output_aliases={5: 0} if aliased else {},
         compiler_params=pltpu.CompilerParams(vmem_limit_bytes=VMEM_BYTES),
         name="correlate",
         cost_estimate=pl.CostEstimate(
@@ -131,32 +156,32 @@
             bytes_accessed=count * width * slots * 2 * half * 2 + 8 * slots * bins,
             transcendentals=0,
         ),
-    )(jnp.stack(places).astype(jnp.int32), *args)
+    )(me, panel, slab, *tables, *([out] if aliased else []))
 
 
 def local(receiver_spectra, source_spectra, quality, slot_order, owners):
     sources, _, bins = source_spectra.shape
     members = lax.axis_size("cross")
     width = sources // members
-    cos_table, sin_table = lag_tables(bins, L)
-    me = lax.axis_index("cross")
-    my_owners = lax.dynamic_index_in_dim(owners, lax.axis_index("blk"), 1, keepdims=False)
-
+    me = lax.axis_index("cross").astype(jnp.int32).reshape(1)
+    mine = lax.dynamic_slice_in_dim(owners, lax.axis_index("blk"), 1, 1)
+
+    shares = lax.all_to_all(source_spectra.reshape(members, width, 2, bins), "cross", 0, 0)
+    tables = lag_tables(bins, L)
     slab0 = prepare(receiver_spectra, quality, slot_order)
-    slab1 = passed_along(slab0, "blk", 1)
-    slabs = [slab0, slab1]
-
-    shares = lax.all_to_all(source_spectra.reshape(members, width, 2, bins), "cross", 0, 0)
-    own = [lax.dynamic_index_in_dim(shares, my_owners[s], 0, keepdims=False) for s in range(STEPS)]
-    chunks = [[own[s]] + [passed_along(own[s], "cross", d) for d in range(1, members)] for s in range(STEPS)]
-    places = [(me - d) % members for d in range(members)]
+    shares, slab0, tables = lax.optimization_barrier((shares, slab0, tables))
+    slabs = [slab0, passed_along(slab0, "blk", 1)]
+
+    own, panels = [], []
+    for s in range(STEPS):
+        share, copies = select(shares, mine[s])
+        own.append(share)
+        panels.append(lax.all_to_all(copies, "cross", 0, 0))
 
     out = None
-    for s, group in [(0, [0]), (0, [1, 2, 3]), (0, [4, 5, 6, 7]), (1, [0, 1, 2, 3, 4, 5, 6, 7])]:
-        out = correlate(
-            out, s, [chunks[s][d] for d in group], [places[d] for d in group],
-            slabs[s], cos_table, sin_table, sources,
-        )
+    for panel_set in (own, panels):
+        for s in range(STEPS):
+            out = correlate(out, s, panel_set[s], me, slabs[s], tables, sources)
     return out[:, None, None]
 
 

time: 131 us -> 102 us (0.78)
  the two profiles are of different devices: /device:TPU:40 before, /device:TPU:1 now
where the time goes in v2:
time: 102 us; the launch traced here: 101 us
  Pallas kernels  61.2 us (60%)
  waiting for transfers between devices  17.4 us (17%)
  starting transfers between devices  17.1 us (17%)
  other arithmetic  2.97 us (3%)
  local copies, waits for them, and re-layouts  2.64 us (3%)
    pallas_call x4, Pallas kernels, correlate(): pl.pallas_call(functools.partial(correlate_kernel, int(aliased)), out_sha...  51.5 us
    all_to_all x1, waiting for transfers between devices, local(): lax.all_to_all(source_spectra.reshape(members, width, 2, bins), 'cross',...  10.1 us
    all_to_all x1, starting transfers between devices, local(): lax.all_to_all(source_spectra.reshape(members, width, 2, bins), 'cross',...  8.29 us
    all_to_all x2, starting transfers between devices, local(): panels.append(lax.all_to_all(copies, 'cross', 0, 0))  7.29 us
    ppermute x1, waiting for transfers between devices, passed_along(): return lax.ppermute(value, axis, pairs)  7.26 us
    pallas_call x2, Pallas kernels, select(): pl.pallas_call(select_kernel, out_shape=(jax.ShapeDtypeStruct(share, F32)...  5.48 us
    pallas_call x1, Pallas kernels, prepare(): pl.pallas_call(prepare_kernel, out_shape=jax.ShapeDtypeStruct((2, slots,...  4.21 us
    convert_element_type x1, other arithmetic, lag_tables(): sin_table = (-jnp.sin(phase_angle) / bins).astype(BF16)  2.96 us
  transfers between devices with their start and end apart: 4, of which 2 were waited for; matrix products, arithmetic and copies ran while one was open for 4% of the time, Pallas kernels for 40%

profile of v2, /device:TPU:1, one launch (start us, length us, event | category | flops | bytes accessed | tf_op | source)
XLA Modules:
  0.0 101.3 jit_solution(355754403676588311)
XLA Ops:
  0.0 0.0 copy-start
  0.0 8.3 %all-to-all-start = ((f32[8,16,2,1024]{3,2,1,0:T(2,128)}), f32[8,16,2,1024]{3,2,1,0:T(2,128)S(1)}, u32[]{:S(2)}, u32[]{:S(2)}) async-start(f32[8,16,2,1024]{3,2,1,0:T(2,128)} %bitcast.7), calls=%async_computation | async-start | bytes 2097152 | tf_op jit(solution)/shard_map/all_to_all | solution.py:169
  8.3 4.2 %prepare.1.slab_ref = f32[2,128,1024]{2,1,0:T(8,128)} custom-call(s32[1,128]{1,0:T(1,128)} %order_ref.1, s32[128]{0:T(128)} %quality_ref.1, f32[128,2,1024]{2,1,0:T(2,128)} %raw_ref.1), custom_call_target="tpu_custom_call" | custom-call | flops 1310720 | bytes 2097152 | tf_op jit(solution)/shard_map/prepare/pallas_call | solution.py:61
  12.5 3.0 %multiply_convert_fusion = (bf16[1024,128]{1,0:T(8,128)(2,1)}, bf16[1024,128]{1,0:T(8,128)(2,1)}) fusion(s32[128]{0:T(128)S(1)} %multiply_add_fusion), kind=kLoop, calls=%fused_computation.6 | loop fusion | flops 2490368 | bytes 524800 | tf_op jit(solution)/shard_map/convert_element_type | solution.py:31
  15.5 10.1 %all-to-all-done.raw_ref = f32[8,16,2,1024]{3,2,1,0:T(2,128)S(1)} async-done(((f32[8,16,2,1024]{3,2,1,0:T(2,128)}), f32[8,16,2,1024]{3,2,1,0:T(2,128)S(1)}, u32[]{:S(2)}, u32[]{:S(2)}) %all-to-all-start) | async-done | bytes 1048608 | tf_op jit(solution)/shard_map/all_to_all | solution.py:169
  25.6 0.0 copy-start.1
  25.6 1.5 %collective-permute-start = (f32[2,128,1024]{2,1,0:T(8,128)}, f32[2,128,1024]{2,1,0:T(8,128)S(1)}, u32[]{:S(2)}, u32[]{:S(2)}) collective-permute-start(f32[2,128,1024]{2,1,0:T(8,128)} %prepare.1.slab_ref), channel_id=1, source_target_pairs={{0,8},{8,16},{16,24},{24,32},{32,40},{40,48},{48,56},{56,64},{64,7... | collective-permute-start | bytes 3145736 | tf_op jit(solution)/shard_map/ppermute | solution.py:22
  27.1 0.0 copy-done
  27.1 0.1 constant_dynamic-slice_fusion
  27.2 0.6 fusion.6
  27.7 0.0 copy-done.1
  27.7 2.8 %select.5 = (f32[16,2,1024]{2,1,0:T(2,128)}, f32[8,16,2,1024]{3,2,1,0:T(2,128)}) custom-call(s32[1]{0:T(128)} %bitcast.3.mine_ref, f32[8,16,2,1024]{3,2,1,0:T(2,128)} %copy-done.1), custom_call_target="tpu_custom_call" | custom-call | tf_op jit(solution)/shard_map/select/pallas_call | solution.py:89
  30.5 3.6 %all-to-all-start.2 = ((f32[8,16,2,1024]{3,2,1,0:T(2,128)}), f32[8,16,2,1024]{3,2,1,0:T(2,128)S(1)}, u32[]{:S(2)}, u32[]{:S(2)}) async-start(f32[8,16,2,1024]{3,2,1,0:T(2,128)} %get-tuple-element.18), calls=%async_computation.2 | async-start | bytes 2097152 | tf_op jit(solution)/shard_map/all_to_all | solution.py:179
  34.1 2.7 %select.4 = (f32[16,2,1024]{2,1,0:T(2,128)}, f32[8,16,2,1024]{3,2,1,0:T(2,128)}) custom-call(s32[1]{0:T(128)} %bitcast.1.mine_ref, f32[8,16,2,1024]{3,2,1,0:T(2,128)} %copy-done.1), custom_call_target="tpu_custom_call" | custom-call | tf_op jit(solution)/shard_map/select/pallas_call | solution.py:89
  36.8 5.0 %correlate.4.refs_0_ = bf16[2,128,128,256]{3,2,1,0:T(8,128)(2,1)} custom-call(s32[1]{0:T(128)} %bitcast.place_ref, f32[16,2,1024]{2,1,0:T(2,128)} %get-tuple-element.20.panel_ref, f32[2,128,1024]{2,1,0:T(8,128)} %prepare.1.slab_ref, bf16[1024,128]{1,0:T(8,128)(2,1)} %get-tuple-element.16.cos_ref, bf16[1024,128]{1,0:T(8,128)(2,1)} %get-tuple-element.17.sin_ref), custom_call_target="tpu_custom_call" | custom-call | flops 2147483648 | bytes 2097152 | tf_op jit(solution)/shard_map/correlate/pallas_call | solution.py:147
  41.7 7.3 %collective-permute-done.slab_ref = f32[2,128,1024]{2,1,0:T(8,128)S(1)} collective-permute-done((f32[2,128,1024]{2,1,0:T(8,128)}, f32[2,128,1024]{2,1,0:T(8,128)S(1)}, u32[]{:S(2)}, u32[]{:S(2)}) %collective-permute-start) | collective-permute-done | bytes 1048608 | tf_op jit(solution)/shard_map/ppermute | solution.py:22
  49.0 0.0 copy-start.2
  49.0 1.0 copy-done.2
  50.0 5.0 %correlate.5.refs_0_ = bf16[2,128,128,256]{3,2,1,0:T(8,128)(2,1)} custom-call(s32[1]{0:T(128)} %bitcast.place_ref, f32[16,2,1024]{2,1,0:T(2,128)} %get-tuple-element.19.panel_ref, f32[2,128,1024]{2,1,0:T(8,128)} %copy-done.2, bf16[1024,128]{1,0:T(8,128)(2,1)} %get-tuple-element.16.cos_ref, ...), custom_call_target="tpu_custom_call", output_to_operand_aliasing={{}: (5, {})} | custom-call | flops 2147483648 | bytes 2097152 | tf_op jit(solution)/shard_map/correlate/pallas_call | solution.py:147
  55.0 0.0 all-to-all-done.2.panel_ref
  55.0 0.0 copy-start.3
  55.0 3.7 %all-to-all-start.1 = ((f32[8,16,2,1024]{3,2,1,0:T(2,128)}), f32[8,16,2,1024]{3,2,1,0:T(2,128)S(1)}, u32[]{:S(2)}, u32[]{:S(2)}) async-start(f32[8,16,2,1024]{3,2,1,0:T(2,128)} %get-tuple-element.14), calls=%async_computation.1 | async-start | bytes 2097152 | tf_op jit(solution)/shard_map/all_to_all | solution.py:179
  58.7 0.0 copy-done.3
  58.7 20.8 %correlate.6.refs_0_ = bf16[2,128,128,256]{3,2,1,0:T(8,128)(2,1)} custom-call(s32[1]{0:T(128)} %bitcast.place_ref, f32[8,16,2,1024]{3,2,1,0:T(2,128)} %copy-done.3, f32[2,128,1024]{2,1,0:T(8,128)} %prepare.1.slab_ref, bf16[1024,128]{1,0:T(8,128)(2,1)} %get-tuple-element.16.cos_ref, ...), custom_call_target="tpu_custom_call", output_to_operand_aliasing={{}: (5, {})} | custom-call | flops 15032385536 | bytes 8388608 | tf_op jit(solution)/shard_map/correlate/pallas_call | solution.py:147
  79.5 0.0 all-to-all-done.1.panel_ref
  79.5 0.0 copy-start.4
  79.5 1.0 copy-done.4
  80.5 20.8 %correlate.7 = bf16[2,128,128,256]{3,2,1,0:T(8,128)(2,1)} custom-call(s32[1]{0:T(128)} %bitcast.place_ref, f32[8,16,2,1024]{3,2,1,0:T(2,128)} %copy-done.4, f32[2,128,1024]{2,1,0:T(8,128)} %copy-done.2, bf16[1024,128]{1,0:T(8,128)(2,1)} %get-tuple-element.16.cos_ref, bf16[1024,128]{1,0:T(8,128)(2,1)} %get-tuple-element.17.sin_ref, ...), custom_call_target="tpu_custom_call", output_to_operand_aliasing={{}: (5, {})} | custom-call | flops 15032385536 | bytes 8388608 | tf_op jit(solution)/shard_map/correlate/pallas_call | solution.py:147
  (1 shorter events, 0.0 us)
Async XLA Ops:
  0.0 27.1 %copy-start = (s32[2,16]{1,0:T(2,128)S(1)}, s32[2,16]{1,0:T(2,128)}, u32[]{:S(2)}) copy-start(s32[2,16]{1,0:T(2,128)} %param.9) | copy-start | bytes 388
  0.0 25.6 %all-to-all-start = ((f32[8,16,2,1024]{3,2,1,0:T(2,128)}), f32[8,16,2,1024]{3,2,1,0:T(2,128)S(1)}, u32[]{:S(2)}, u32[]{:S(2)}) async-start(f32[8,16,2,1024]{3,2,1,0:T(2,128)} %bitcast.7), calls=%async_computation | async-start | bytes 2097152 | tf_op jit(solution)/shard_map/all_to_all | solution.py:169
  25.6 2.1 %copy-start.1 = (f32[8,16,2,1024]{3,2,1,0:T(2,128)}, f32[8,16,2,1024]{3,2,1,0:T(2,128)S(1)}, u32[]{:S(2)}) copy-start(f32[8,16,2,1024]{3,2,1,0:T(2,128)S(1)} %all-to-all-done.raw_ref) | copy-start | bytes 3145732
  25.6 23.4 %collective-permute-start = (f32[2,128,1024]{2,1,0:T(8,128)}, f32[2,128,1024]{2,1,0:T(8,128)S(1)}, u32[]{:S(2)}, u32[]{:S(2)}) collective-permute-start(f32[2,128,1024]{2,1,0:T(8,128)} %prepare.1.slab_ref), channel_id=1, source_target_pairs={{0,8},{8,16},{16,24},{24,32},{32,40},{40,48},{48,56},{56,64},{64,7... | collective-permute-start | bytes 3145736 | tf_op jit(solution)/shard_map/ppermute | solution.py:22
  30.5 24.5 %all-to-all-start.2 = ((f32[8,16,2,1024]{3,2,1,0:T(2,128)}), f32[8,16,2,1024]{3,2,1,0:T(2,128)S(1)}, u32[]{:S(2)}, u32[]{:S(2)}) async-start(f32[8,16,2,1024]{3,2,1,0:T(2,128)} %get-tuple-element.18), calls=%async_computation.2 | async-start | bytes 2097152 | tf_op jit(solution)/shard_map/all_to_all | solution.py:179
  49.0 1.0 copy-start.2
  55.0 3.8 %copy-start.3 = (f32[8,16,2,1024]{3,2,1,0:T(2,128)}, f32[8,16,2,1024]{3,2,1,0:T(2,128)S(1)}, u32[]{:S(2)}) copy-start(f32[8,16,2,1024]{3,2,1,0:T(2,128)S(1)} %all-to-all-done.2.panel_ref) | copy-start | bytes 3145732
  55.0 24.6 %all-to-all-start.1 = ((f32[8,16,2,1024]{3,2,1,0:T(2,128)}), f32[8,16,2,1024]{3,2,1,0:T(2,128)S(1)}, u32[]{:S(2)}, u32[]{:S(2)}) async-start(f32[8,16,2,1024]{3,2,1,0:T(2,128)} %get-tuple-element.14), calls=%async_computation.1 | async-start | bytes 2097152 | tf_op jit(solution)/shard_map/all_to_all | solution.py:179
  79.5 1.0 copy-start.4

commit v3 on v2

--- a/solution.py
+++ b/solution.py
@@ -102,33 +102,29 @@
     )(owner, shares)
 
 
-def correlate_kernel(aliased, place_ref, panel_ref, slab_ref, cos_ref, sin_ref, *refs):
+def correlate_kernel(aliased, place_ref, panel_ref, slab_ref, table_ref, *refs):
     out_ref = refs[aliased]
     width = panel_ref.shape[0]
-    slots = slab_ref.shape[1]
-    half = cos_ref.shape[1]
+    slots, bins = slab_ref.shape[1:]
+    group = math.gcd(width, 8)
     slab_re, slab_im = slab_ref[0], slab_ref[1]
-    inphase, quadrature = [], []
-    for p in range(width):
-        pair = panel_ref[p]
-        re, im = pair[0:1, :], pair[1:2, :]
-        inphase.append((re * slab_re + im * slab_im).astype(BF16))
-        quadrature.append((im * slab_re - re * slab_im).astype(BF16))
-    inphase = jnp.concatenate(inphase, axis=0)
-    quadrature = jnp.concatenate(quadrature, axis=0)
-    even = jnp.dot(inphase, cos_ref[...], preferred_element_type=F32)
-    odd = jnp.dot(quadrature, sin_ref[...], preferred_element_type=F32)
-    for p in range(width):
-        e = even[p * slots : (p + 1) * slots]
-        o = odd[p * slots : (p + 1) * slots]
-        out_ref[p, :, :half] = (e + o).astype(BF16)
-        out_ref[p, :, half:] = (e - o).astype(BF16)
-
-
-def correlate(out, step, panel, me, slab, tables, sources):
+    for first in range(0, width, group):
+        rows = []
+        for p in range(first, first + group):
+            pair = panel_ref[p]
+            re, im = pair[0:1, :], pair[1:2, :]
+            inphase = (re * slab_re + im * slab_im).astype(BF16)
+            quadrature = (im * slab_re - re * slab_im).astype(BF16)
+            rows.append(jnp.concatenate([inphase, quadrature], axis=1))
+        sums = jnp.dot(jnp.concatenate(rows, axis=0), table_ref[...], preferred_element_type=F32)
+        for p in range(group):
+            out_ref[first + p] = sums[p * slots : (p + 1) * slots].astype(BF16)
+
+
+def correlate(out, step, panel, me, slab, table, sources):
     width, _, bins = panel.shape[-3:]
     slots = slab.shape[1]
-    half = tables[0].shape[1]
+    lags = table.shape[1]
     aliased = out is not None
     if panel.ndim == 3:
         count = 1
@@ -141,22 +137,22 @@
     grid_spec = pltpu.PrefetchScalarGridSpec(
         num_scalar_prefetch=1,
         grid=(count,),
-        in_specs=[panel_spec, VMEM, VMEM, VMEM] + ([pl.BlockSpec(memory_space=pl.ANY)] if aliased else []),
-        out_specs=pl.BlockSpec((None, width, slots, 2 * half), lambda i, mine: (step, place(i, mine), 0, 0)),
+        in_specs=[panel_spec, VMEM, VMEM] + ([pl.BlockSpec(memory_space=pl.ANY)] if aliased else []),
+        out_specs=pl.BlockSpec((None, width, slots, lags), lambda i, mine: (step, place(i, mine), 0, 0)),
     )
     return pl.pallas_call(
         functools.partial(correlate_kernel, int(aliased)),
-        out_shape=jax.ShapeDtypeStruct((STEPS, sources, slots, 2 * half), BF16),
+        out_shape=jax.ShapeDtypeStruct((STEPS, sources, slots, lags), BF16),
         grid_spec=grid_spec,
-        input_output_aliases={5: 0} if aliased else {},
+        input_output_aliases={4: 0} if aliased else {},
         compiler_params=pltpu.CompilerParams(vmem_limit_bytes=VMEM_BYTES),
         name="correlate",
         cost_estimate=pl.CostEstimate(
-            flops=count * width * slots * bins * 4 * 2 * half,
-            bytes_accessed=count * width * slots * 2 * half * 2 + 8 * slots * bins,
+            flops=count * width * slots * bins * 4 * lags,
+            bytes_accessed=count * width * slots * lags * 2 + 8 * slots * bins,
             transcendentals=0,
         ),
-    )(me, panel, slab, *tables, *([out] if aliased else []))
+    )(me, panel, slab, table, *([out] if aliased else []))
 
 
 def local(receiver_spectra, source_spectra, quality, slot_order, owners):
@@ -167,21 +163,26 @@
     mine = lax.dynamic_slice_in_dim(owners, lax.axis_index("blk"), 1, 1)
 
     shares = lax.all_to_all(source_spectra.reshape(members, width, 2, bins), "cross", 0, 0)
-    tables = lag_tables(bins, L)
+    cos_table, sin_table = lag_tables(bins, L)
+    table = jnp.concatenate(
+        [jnp.concatenate([cos_table, cos_table], axis=1), jnp.concatenate([sin_table, -sin_table], axis=1)], axis=0
+    )
     slab0 = prepare(receiver_spectra, quality, slot_order)
-    shares, slab0, tables = lax.optimization_barrier((shares, slab0, tables))
-    slabs = [slab0, passed_along(slab0, "blk", 1)]
-
-    own, panels = [], []
-    for s in range(STEPS):
-        share, copies = select(shares, mine[s])
-        own.append(share)
-        panels.append(lax.all_to_all(copies, "cross", 0, 0))
-
-    out = None
-    for panel_set in (own, panels):
-        for s in range(STEPS):
-            out = correlate(out, s, panel_set[s], me, slabs[s], tables, sources)
+    owner0, owner1 = mine[0], mine[1]
+    shares, slab0, table, me, owner0, owner1 = lax.optimization_barrier(
+        (shares, slab0, table, me, owner0, owner1)
+    )
+
+    own0, copies0 = select(shares, owner0)
+    own1, copies1 = select(shares, owner1)
+    panel0 = lax.all_to_all(copies0, "cross", 0, 0)
+    slab1 = passed_along(slab0, "blk", 1)
+    panel1 = lax.all_to_all(copies1, "cross", 0, 0)
+
+    out = correlate(None, 0, own0, me, slab0, table, sources)
+    out = correlate(out, 1, own1, me, slab1, table, sources)
+    out = correlate(out, 0, panel0, me, slab0, table, sources)
+    out = correlate(out, 1, panel1, me, slab1, table, sources)
     return out[:, None, None]
 
 

time: 102 us -> 98.2 us (0.963)
  Pallas kernels: 61.2 us -> 58.1 us
  waiting for transfers between devices: 17.4 us -> 14.5 us
  other arithmetic: 2.97 us -> 5.32 us
    pallas_call x4, Pallas kernels: 51.5 us -> 48.2 us  [correlate(): pl.pallas_call(functools.partial(correlate_kernel, int(aliased)), out_sha...]
    all_to_all x1, waiting for transfers between devices: 10.1 us -> 7.08 us  [local(): lax.all_to_all(source_spectra.reshape(members, width, 2, bins), 'cross',...]
    neg x0 -> x1, other arithmetic: none -> 2 us  [local(): -sin_table]
    concatenate x0 -> x1, other arithmetic: none -> 1.07 us  [local(): jnp.concatenate([jnp.concatenate([cos_table, cos_table], axis=1), jnp.con...]
  transfers between devices with their start and end apart: 4 -> 4, of which waited for: 2 -> 2; matrix products, arithmetic and copies ran while one was open for 4% -> 6% of each run, Pallas kernels for 40% -> 40%
where the time goes in v3:
time: 98.2 us; the launch traced here: 97.7 us
  Pallas kernels  58.1 us (59%)
  starting transfers between devices  17.1 us (17%)
  waiting for transfers between devices  14.5 us (15%)
  other arithmetic  5.32 us (5%)
  local copies, waits for them, and re-layouts  2.64 us (3%)
    pallas_call x4, Pallas kernels, correlate(): pl.pallas_call(functools.partial(correlate_kernel, int(aliased)), out_sha...  48.2 us
    all_to_all x1, starting transfers between devices, local(): lax.all_to_all(source_spectra.reshape(members, width, 2, bins), 'cross',...  8.29 us
    ppermute x1, waiting for transfers between devices, passed_along(): return lax.ppermute(value, axis, pairs)  7.44 us
    all_to_all x1, waiting for transfers between devices, local(): lax.all_to_all(source_spectra.reshape(members, width, 2, bins), 'cross',...  7.08 us
    pallas_call x2, Pallas kernels, select(): pl.pallas_call(select_kernel, out_shape=(jax.ShapeDtypeStruct(share, F32)...  5.67 us
    pallas_call x1, Pallas kernels, prepare(): pl.pallas_call(prepare_kernel, out_shape=jax.ShapeDtypeStruct((2, slots,...  4.22 us
    all_to_all x1, starting transfers between devices, local(): panel1 = lax.all_to_all(copies1, 'cross', 0, 0)  3.74 us
    all_to_all x1, starting transfers between devices, local(): panel0 = lax.all_to_all(copies0, 'cross', 0, 0)  3.56 us
  transfers between devices with their start and end apart: 4, of which 2 were waited for; matrix products, arithmetic and copies ran while one was open for 6% of the time, Pallas kernels for 40%

profile of v3, /device:TPU:1, one launch (start us, length us, event | category | flops | bytes accessed | tf_op | source)
XLA Modules:
  0.0 97.7 jit_solution(16262563641171219715)
XLA Ops:
  0.0 0.0 copy-start
  0.0 8.3 %all-to-all-start = ((f32[8,16,2,1024]{3,2,1,0:T(2,128)}), f32[8,16,2,1024]{3,2,1,0:T(2,128)S(1)}, u32[]{:S(2)}, u32[]{:S(2)}) async-start(f32[8,16,2,1024]{3,2,1,0:T(2,128)} %bitcast.7), calls=%async_computation | async-start | bytes 2097152 | tf_op jit(solution)/shard_map/all_to_all | solution.py:165
  8.3 0.0 copy-done
  8.3 0.1 constant_dynamic-slice_fusion
  8.4 4.2 %prepare.1.slab_ref = f32[2,128,1024]{2,1,0:T(8,128)} custom-call(s32[1,128]{1,0:T(1,128)} %order_ref.1, s32[128]{0:T(128)} %quality_ref.1, f32[128,2,1024]{2,1,0:T(2,128)} %raw_ref.1), custom_call_target="tpu_custom_call" | custom-call | flops 1310720 | bytes 2097152 | tf_op jit(solution)/shard_map/prepare/pallas_call | solution.py:61
  12.6 0.0 copy-start.2
  12.6 0.6 fusion.7
  13.2 2.0 %fusion.6 = bf16[1024,128]{1,0:T(8,128)(2,1)S(1)} fusion(s32[128]{0:T(128)S(1)} %multiply_add_fusion), kind=kLoop, calls=%fused_computation.12 | loop fusion | flops 2621440 | bytes 262656 | tf_op jit(solution)/shard_map/neg | solution.py:168
  15.2 2.2 %multiply_convert_fusion.1 = (bf16[1024,128]{1,0:T(8,128)(2,1)S(1)}, bf16[1024,128]{1,0:T(8,128)(2,1)S(1)}) fusion(s32[128]{0:T(128)S(1)} %multiply_add_fusion), kind=kLoop, calls=%fused_computation.8 | loop fusion | flops 2490368 | bytes 524800 | tf_op jit(solution)/shard_map/convert_element_type | solution.py:30
  17.5 1.1 %maximum_maximum_fusion.table_ref = bf16[2048,256]{1,0:T(8,128)(2,1)} fusion(bf16[1024,128]{1,0:T(8,128)(2,1)S(1)} %fusion.6, bf16[1024,128]{1,0:T(8,128)(2,1)S(1)} %get-tuple-element.28, bf16[1024,128]{1,0:T(8,128)(2,1)S(1)} %get-tuple-element.27), kind=kLoop, calls=%fused_computation | loop fusion | flops 4194304 | bytes 1835008 | tf_op jit(solution)/shard_map/concatenate | solution.py:167
  18.5 7.1 %all-to-all-done.raw_ref = f32[8,16,2,1024]{3,2,1,0:T(2,128)S(1)} async-done(((f32[8,16,2,1024]{3,2,1,0:T(2,128)}), f32[8,16,2,1024]{3,2,1,0:T(2,128)S(1)}, u32[]{:S(2)}, u32[]{:S(2)}) %all-to-all-start) | async-done | bytes 1048608 | tf_op jit(solution)/shard_map/all_to_all | solution.py:165
  25.6 0.0 copy-start.1
  25.6 0.0 copy-done.2
  25.6 1.5 %collective-permute-start = (f32[2,128,1024]{2,1,0:T(8,128)S(1)}, f32[2,128,1024]{2,1,0:T(8,128)S(1)}, u32[]{:S(2)}, u32[]{:S(2)}) collective-permute-start(f32[2,128,1024]{2,1,0:T(8,128)S(1)} %copy-done.2), channel_id=1, source_target_pairs={{0,8},{8,16},{16,24},{24,32},{32,40},{40,48},{48,56},{56,64},{64,7... | collective-permute-start | bytes 3145736 | tf_op jit(solution)/shard_map/ppermute | solution.py:22
  27.1 0.0 copy-done.1
  27.1 2.8 %select.5 = (f32[16,2,1024]{2,1,0:T(2,128)}, f32[8,16,2,1024]{3,2,1,0:T(2,128)}) custom-call(s32[1]{0:T(128)} %bitcast.2.mine_ref, f32[8,16,2,1024]{3,2,1,0:T(2,128)} %copy-done.1), custom_call_target="tpu_custom_call" | custom-call | tf_op jit(solution)/shard_map/select/pallas_call | solution.py:89
  29.9 3.6 %all-to-all-start.2 = ((f32[8,16,2,1024]{3,2,1,0:T(2,128)}), f32[8,16,2,1024]{3,2,1,0:T(2,128)S(1)}, u32[]{:S(2)}, u32[]{:S(2)}) async-start(f32[8,16,2,1024]{3,2,1,0:T(2,128)} %get-tuple-element.22), calls=%async_computation.2 | async-start | bytes 2097152 | tf_op jit(solution)/shard_map/all_to_all | solution.py:178
  33.4 2.9 %select.4 = (f32[16,2,1024]{2,1,0:T(2,128)}, f32[8,16,2,1024]{3,2,1,0:T(2,128)}) custom-call(s32[1]{0:T(128)} %bitcast.3.mine_ref, f32[8,16,2,1024]{3,2,1,0:T(2,128)} %copy-done.1), custom_call_target="tpu_custom_call" | custom-call | tf_op jit(solution)/shard_map/select/pallas_call | solution.py:89
  36.3 4.9 %correlate.4.refs_0_ = bf16[2,128,128,256]{3,2,1,0:T(8,128)(2,1)} custom-call(s32[1]{0:T(128)} %bitcast.1.place_ref, f32[16,2,1024]{2,1,0:T(2,128)} %get-tuple-element.24.panel_ref, f32[2,128,1024]{2,1,0:T(8,128)} %prepare.1.slab_ref, bf16[2048,256]{1,0:T(8,128)(2,1)} %maximum_maximum_fusion.table_ref), custom_call_target="tpu_custom_call" | custom-call | flops 2147483648 | bytes 2097152 | tf_op jit(solution)/shard_map/correlate/pallas_call | solution.py:143
  41.2 7.4 %collective-permute-done.slab_ref = f32[2,128,1024]{2,1,0:T(8,128)S(1)} collective-permute-done((f32[2,128,1024]{2,1,0:T(8,128)S(1)}, f32[2,128,1024]{2,1,0:T(8,128)S(1)}, u32[]{:S(2)}, u32[]{:S(2)}) %collective-permute-start) | collective-permute-done | bytes 1048608 | tf_op jit(solution)/shard_map/ppermute | solution.py:22
  48.7 0.0 copy-start.3
  48.7 1.0 copy-done.3
  49.6 4.9 %correlate.5.refs_0_ = bf16[2,128,128,256]{3,2,1,0:T(8,128)(2,1)} custom-call(s32[1]{0:T(128)} %bitcast.1.place_ref, f32[16,2,1024]{2,1,0:T(2,128)} %get-tuple-element.23.panel_ref, f32[2,128,1024]{2,1,0:T(8,128)} %copy-done.3, bf16[2048,256]{1,0:T(8,128)(2,1)} %maximum_maximum_fusion.table_ref, ...), custom_call_target="tpu_custom_call", output_to_operand_aliasing={{}: (4, {})} | custom-call | flops 2147483648 | bytes 2097152 | tf_op jit(solution)/shard_map/correlate/pallas_call | solution.py:143
  54.5 0.0 all-to-all-done.2.panel_ref
  54.5 0.0 copy-start.4
  54.5 3.7 %all-to-all-start.1 = ((f32[8,16,2,1024]{3,2,1,0:T(2,128)}), f32[8,16,2,1024]{3,2,1,0:T(2,128)S(1)}, u32[]{:S(2)}, u32[]{:S(2)}) async-start(f32[8,16,2,1024]{3,2,1,0:T(2,128)} %get-tuple-element.18), calls=%async_computation.1 | async-start | bytes 2097152 | tf_op jit(solution)/shard_map/all_to_all | solution.py:180
  58.3 0.0 copy-done.4
  58.3 19.2 %correlate.6.refs_0_ = bf16[2,128,128,256]{3,2,1,0:T(8,128)(2,1)} custom-call(s32[1]{0:T(128)} %bitcast.1.place_ref, f32[8,16,2,1024]{3,2,1,0:T(2,128)} %copy-done.4, f32[2,128,1024]{2,1,0:T(8,128)} %prepare.1.slab_ref, bf16[2048,256]{1,0:T(8,128)(2,1)} %maximum_maximum_fusion.table_ref, ...), custom_call_target="tpu_custom_call", output_to_operand_aliasing={{}: (4, {})} | custom-call | flops 15032385536 | bytes 8388608 | tf_op jit(solution)/shard_map/correlate/pallas_call | solution.py:143
  77.5 0.0 all-to-all-done.1.panel_ref
  77.5 0.0 copy-start.5
  77.5 1.0 %copy-done.5 = f32[8,16,2,1024]{3,2,1,0:T(2,128)} copy-done((f32[8,16,2,1024]{3,2,1,0:T(2,128)}, f32[8,16,2,1024]{3,2,1,0:T(2,128)S(1)}, u32[]{:S(2)}) %copy-start.5) | copy-done | bytes 1048600
  78.5 19.2 %correlate.7 = bf16[2,128,128,256]{3,2,1,0:T(8,128)(2,1)} custom-call(s32[1]{0:T(128)} %bitcast.1.place_ref, f32[8,16,2,1024]{3,2,1,0:T(2,128)} %copy-done.5, f32[2,128,1024]{2,1,0:T(8,128)} %copy-done.3, bf16[2048,256]{1,0:T(8,128)(2,1)} %maximum_maximum_fusion.table_ref, bf16[2,128,128,256]{3,2,1,0:T(8,128)(2,1)} %correlate.6.refs_0_), custom_call_target="tpu_custom_call", output_to_operand_aliasing={{}: (4, {})} | custom-call | flops 15032385536 | bytes 8388608 | tf_op jit(solution)/shard_map/correlate/pallas_call | solution.py:143
  (1 shorter events, 0.0 us)
Async XLA Ops:
  0.0 8.3 %copy-start = (s32[2,16]{1,0:T(2,128)S(1)}, s32[2,16]{1,0:T(2,128)}, u32[]{:S(2)}) copy-start(s32[2,16]{1,0:T(2,128)} %param.9) | copy-start | bytes 388
  0.0 25.6 %all-to-all-start = ((f32[8,16,2,1024]{3,2,1,0:T(2,128)}), f32[8,16,2,1024]{3,2,1,0:T(2,128)S(1)}, u32[]{:S(2)}, u32[]{:S(2)}) async-start(f32[8,16,2,1024]{3,2,1,0:T(2,128)} %bitcast.7), calls=%async_computation | async-start | bytes 2097152 | tf_op jit(solution)/shard_map/all_to_all | solution.py:165
  12.6 13.0 %copy-start.2 = (f32[2,128,1024]{2,1,0:T(8,128)S(1)}, f32[2,128,1024]{2,1,0:T(8,128)}, u32[]{:S(2)}) copy-start(f32[2,128,1024]{2,1,0:T(8,128)} %prepare.1.slab_ref) | copy-start | bytes 3145732
  25.6 1.5 %copy-start.1 = (f32[8,16,2,1024]{3,2,1,0:T(2,128)}, f32[8,16,2,1024]{3,2,1,0:T(2,128)S(1)}, u32[]{:S(2)}) copy-start(f32[8,16,2,1024]{3,2,1,0:T(2,128)S(1)} %all-to-all-done.raw_ref) | copy-start | bytes 3145732
  25.6 23.0 %collective-permute-start = (f32[2,128,1024]{2,1,0:T(8,128)S(1)}, f32[2,128,1024]{2,1,0:T(8,128)S(1)}, u32[]{:S(2)}, u32[]{:S(2)}) collective-permute-start(f32[2,128,1024]{2,1,0:T(8,128)S(1)} %copy-done.2), channel_id=1, source_target_pairs={{0,8},{8,16},{16,24},{24,32},{32,40},{40,48},{48,56},{56,64},{64,7... | collective-permute-start | bytes 3145736 | tf_op jit(solution)/shard_map/ppermute | solution.py:22
  29.9 24.7 %all-to-all-start.2 = ((f32[8,16,2,1024]{3,2,1,0:T(2,128)}), f32[8,16,2,1024]{3,2,1,0:T(2,128)S(1)}, u32[]{:S(2)}, u32[]{:S(2)}) async-start(f32[8,16,2,1024]{3,2,1,0:T(2,128)} %get-tuple-element.22), calls=%async_computation.2 | async-start | bytes 2097152 | tf_op jit(solution)/shard_map/all_to_all | solution.py:178
  48.7 1.0 copy-start.3
  54.5 3.8 %copy-start.4 = (f32[8,16,2,1024]{3,2,1,0:T(2,128)}, f32[8,16,2,1024]{3,2,1,0:T(2,128)S(1)}, u32[]{:S(2)}) copy-start(f32[8,16,2,1024]{3,2,1,0:T(2,128)S(1)} %all-to-all-done.2.panel_ref) | copy-start | bytes 3145732
  54.5 23.0 %all-to-all-start.1 = ((f32[8,16,2,1024]{3,2,1,0:T(2,128)}), f32[8,16,2,1024]{3,2,1,0:T(2,128)S(1)}, u32[]{:S(2)}, u32[]{:S(2)}) async-start(f32[8,16,2,1024]{3,2,1,0:T(2,128)} %get-tuple-element.18), calls=%async_computation.1 | async-start | bytes 2097152 | tf_op jit(solution)/shard_map/all_to_all | solution.py:180
  77.5 1.0 %copy-start.5 = (f32[8,16,2,1024]{3,2,1,0:T(2,128)}, f32[8,16,2,1024]{3,2,1,0:T(2,128)S(1)}, u32[]{:S(2)}) copy-start(f32[8,16,2,1024]{3,2,1,0:T(2,128)S(1)} %all-to-all-done.1.panel_ref) | copy-start | bytes 3145732

commit v4 on v3

v4 whole, which is shorter than its diff:
```python
import functools
import math

import jax
import jax.numpy as jnp
from jax import lax
from jax.experimental import pallas as pl
from jax.experimental.pallas import tpu as pltpu
from jax.sharding import PartitionSpec as P

L = 256
STEPS = 2
F32 = jnp.float32
BF16 = jnp.bfloat16
VMEM = pl.BlockSpec(memory_space=pltpu.VMEM)
VMEM_BYTES = 24 << 20
SMALL_VMEM_BYTES = 8 << 20


def passed_along(value, axis, steps):
    count = lax.axis_size(axis)
    pairs = [(source, (source + steps) % count) for source in range(count)]
    return lax.ppermute(value, axis, pairs)


def lag_tables(bins, lags):
    bin_index = jnp.arange(bins, dtype=jnp.int32)
    odd_index = 2 * jnp.arange(lags // 2, dtype=jnp.int32) + 1
    phase_turns = jnp.mod(bin_index[:, None] * odd_index[None, :], 4 * bins).astype(F32)
    phase_angle = phase_turns * (math.pi / (2 * bins))
    cos_table = (jnp.cos(phase_angle) / bins).astype(BF16)
    sin_table = (-jnp.sin(phase_angle) / bins).astype(BF16)
    return (cos_table, sin_table)


def prepare_kernel(order_ref, quality_ref, raw_ref, out_ref):
    slots, _, bins = raw_ref.shape

    def eight(step, _):
        base = pl.multiple_of(step * 8, 8)
        real, imag, kept = [], [], []
        for i in range(8):
            channel = order_ref[0, base + i]
            pair = raw_ref[channel]
            real.append(pair[0:1, :])
            imag.append(pair[1:2, :])
            kept.append(jnp.full((1, 1), quality_ref[channel].astype(F32), F32))
        real = jnp.concatenate(real, axis=0)
        imag = jnp.concatenate(imag, axis=0)
        kept = jnp.concatenate(kept, axis=0)
        power = jnp.sum(real * real + imag * imag, axis=1, keepdims=True) / (2 * bins)
        scale = lax.rsqrt(power + 1e-06)
        out_ref[0, pl.ds(base, 8), :] = real * scale * kept
        out_ref[1, pl.ds(base, 8), :] = imag * scale * kept
        return 0

    lax.fori_loop(0, slots // 8, eight, 0)


def prepare(raw, quality, slot_order):
    slots, _, bins = raw.shape
    return pl.pallas_call(
        prepare_kernel,
        out_shape=jax.ShapeDtypeStruct((2, slots, bins), F32),
        in_specs=[
            pl.BlockSpec(memory_space=pltpu.SMEM),
            pl.BlockSpec(memory_space=pltpu.SMEM),
            VMEM,
        ],
        out_specs=VMEM,
        name="prepare",
        cost_estimate=pl.CostEstimate(flops=5 * raw.size, bytes_accessed=8 * raw.size, transcendentals=0),
    )(slot_order, quality, raw)


def select_kernel(owners_ref, shares_ref, own_ref, raw_ref, white_ref, read_sems, write_sems):
    steps = own_ref.shape[0]
    reads = [pltpu.make_async_copy(shares_ref.at[owners_ref[s, 0]], raw_ref.at[s], read_sems.at[s]) for s in range(steps)]
    writes = [pltpu.make_async_copy(white_ref.at[s], own_ref.at[s], write_sems.at[s]) for s in range(steps)]
    for read in reads:
        read.start()
    for s in range(steps):
        reads[s].wait()
        raw = raw_ref[s]
        count = 2 * raw.shape[2]
        power = jnp.sum(jnp.sum(raw * raw, axis=2, keepdims=True), axis=1, keepdims=True) / count
        white_ref[s] = raw * lax.rsqrt(power + 1e-06)
        writes[s].start()
    for write in writes:
        write.wait()


def select(shares, owners):
    own = (owners.shape[0],) + shares.shape[1:]
    return pl.pallas_call(
        select_kernel,
        out_shape=jax.ShapeDtypeStruct(own, F32),
        in_specs=[pl.BlockSpec(memory_space=pltpu.SMEM), pl.BlockSpec(memory_space=pl.ANY)],
        out_specs=pl.BlockSpec(memory_space=pl.ANY),
        scratch_shapes=[
            pltpu.VMEM(own, F32),
            pltpu.VMEM(own, F32),
            pltpu.SemaphoreType.DMA(own[:1]),
            pltpu.SemaphoreType.DMA(own[:1]),
        ],
        compiler_params=pltpu.CompilerParams(vmem_limit_bytes=SMALL_VMEM_BYTES),
        name="select",
    )(owners, shares)


def correlate_kernel(arrays, aliased, places_ref, *refs):
    panel_refs, (slab_ref, table_ref) = refs[:arrays], refs[arrays : arrays + 2]
    out_ref, shares_ref, sems = refs[arrays + 2 + aliased :]
    width = shares_ref.shape[1]
    slots, bins = slab_ref.shape[1:]
    group = math.gcd(width, 8)
    step = pl.program_id(0)

    @pl.when(step == 0)
    def _():
        slot = 0
        for panel_ref in panel_refs:
            for row in range(panel_ref.shape[0]):
                pltpu.make_async_copy(panel_ref.at[row], shares_ref.at[slot], sems.at[slot]).start()
                slot += 1

    share_ref = shares_ref.at[step]
    pltpu.make_async_copy(panel_refs[0].at[0], share_ref, sems.at[step]).wait()
    slab_re, slab_im = slab_ref[0], slab_ref[1]
    for first in range(0, width, group):
        rows = []
        for p in range(first, first + group):
            pair = share_ref[p]
            re, im = pair[0:1, :], pair[1:2, :]
            inphase = (re * slab_re + im * slab_im).astype(BF16)
            quadrature = (im * slab_re - re * slab_im).astype(BF16)
            rows.append(jnp.concatenate([inphase, quadrature], axis=1))
        sums = jnp.dot(jnp.concatenate(rows, axis=0), table_ref[...], preferred_element_type=F32)
        for p in range(group):
            out_ref[first + p] = sums[p * slots : (p + 1) * slots].astype(BF16)


def correlate(out, step, panels, places, first, slab, table, sources):
    width, _, bins = panels[0].shape[1:]
    slots = slab.shape[1]
    lags = table.shape[1]
    arrays = len(panels)
    count = sum(panel.shape[0] for panel in panels)
    aliased = out is not None
    anywhere = pl.BlockSpec(memory_space=pl.ANY)
    grid_spec = pltpu.PrefetchScalarGridSpec(
        num_scalar_prefetch=1,
        grid=(count,),
        in_specs=[anywhere] * arrays + [VMEM, VMEM] + [anywhere] * aliased,
        out_specs=pl.BlockSpec((None, width, slots, lags), lambda i, members: (step, members[first + i], 0, 0)),
        scratch_shapes=[pltpu.VMEM((count, width, 2, bins), F32), pltpu.SemaphoreType.DMA((count,))],
    )
    return pl.pallas_call(
        functools.partial(correlate_kernel, arrays, int(aliased)),
        out_shape=jax.ShapeDtypeStruct((STEPS, sources, slots, lags), BF16),
        grid_spec=grid_spec,
        input_output_aliases={arrays + 3: 0} if aliased else {},
        compiler_params=pltpu.CompilerParams(vmem_limit_bytes=VMEM_BYTES),
        name="correlate",
        cost_estimate=pl.CostEstimate(
            flops=count * width * slots * bins * 4 * lags,
            bytes_accessed=count * width * slots * lags * 2 + 8 * slots * bins,
            transcendentals=0,
        ),
    )(places, *panels, slab, table, *([out] if aliased else []))


def local(receiver_spectra, source_spectra, quality, slot_order, owners):
    sources, _, bins = source_spectra.shape
    members = lax.axis_size("cross")
    width = sources // members
    row = members // 2
    me = lax.axis_index("cross")
    shifts = [0, 1, row - 1] + list(range(2, row - 1))
    order = jnp.arange(members, dtype=jnp.int32)
    shift = jnp.repeat(jnp.asarray(shifts, jnp.int32), 2)
    places = (me // row + order) % 2 * row + (me % row + row - shift) % row
    mine = lax.dynamic_slice_in_dim(owners, lax.axis_index("blk"), 1, 1)

    shares = lax.all_to_all(source_spectra.reshape(members, width, 2, bins), "cross", 0, 0)
    cos_table, sin_table = lag_tables(bins, L)
    table = jnp.concatenate(
        [jnp.concatenate([cos_table, cos_table], axis=1), jnp.concatenate([sin_table, -sin_table], axis=1)], axis=0
    )
    slab0 = prepare(receiver_spectra, quality, slot_order)
    shares, slab0, table, places, mine = lax.optimization_barrier((shares, slab0, table, places, mine))

    own = select(shares, mine)
    across = [(i, (i + row) % members) for i in range(members)]
    rings = [[(i, i // row * row + (i + d) % row) for i in range(members)] for d in shifts[1:]]

    other0 = lax.ppermute(own[:1], "cross", across)
    pair0 = jnp.concatenate([own[:1], other0], axis=0)
    rest0 = [lax.ppermute(pair0, "cross", ring) for ring in rings]
    other1 = lax.ppermute(own[1:], "cross", across)
    other1, sent = lax.optimization_barrier((other1, slab0))
    slab1 = passed_along(sent, "blk", 1)
    pair1 = jnp.concatenate([own[1:], other1], axis=0)

    out = correlate(None, 0, [own[:1]], places, 0, slab0, table, sources)
    out = correlate(out, 0, [other0], places, 1, slab0, table, sources)
    out, pair1 = lax.optimization_barrier((out, pair1))
    rest1 = [lax.ppermute(pair1, "cross", ring) for ring in rings]
    out = correlate(out, 0, rest0, places, 2, slab0, table, sources)
    out = correlate(out, 1, [pair1] + rest1, places, 0, slab1, table, sources)
    return out[:, None, None]


def solution(mesh):
    placed = (
        P(("blk", "cross"), None, None),
        P(("blk", "cross"), None, None),
        P(("blk", "cross")),
        P(("blk", "cross"), None),
        P(),
    )
    return jax.shard_map(
        local,
        mesh=mesh,
        in_specs=placed,
        out_specs=P(None, "blk", "cross", None, None, None),
        check_vma=False,
    )
```

time: 98.2 us -> 91.4 us (0.931)
  starting transfers between devices: 17.1 us -> 23.8 us
  waiting for transfers between devices: 14.5 us -> 8.46 us
  Pallas kernels: 58.1 us -> 53.7 us
  local copies, waits for them, and re-layouts: 2.64 us -> 0.26 us
    ppermute x0 -> x8, starting transfers between devices: none -> 10.3 us  [the longest x3 4.5 us: local(): rest1 = [lax.ppermute(pair1, 'cross', ring) for ring in rings]]
    ppermute x1, waiting for transfers between devices: 7.44 us -> 0.01 us  [passed_along(): return lax.ppermute(value, axis, pairs)]
    all_to_all x2 -> x0, starting transfers between devices: 7.29 us -> none  [the longest x1 3.74 us: local(): panel1 = lax.all_to_all(copies1, 'cross', 0, 0)]
    pallas_call x6 -> x5, Pallas kernels: 53.9 us -> 49.5 us  [the longest x4 48 us: correlate(): pl.pallas_call(functools.partial(correlate_kernel, arrays, int(aliased)),...]
    ppermute x1, starting transfers between devices: 1.47 us -> 5.17 us  [passed_along(): return lax.ppermute(value, axis, pairs)]
    unnamed x12 -> x6, local copies, waits for them, and re-layouts: 1.97 us -> 0.01 us
    all_to_all x1, waiting for transfers between devices: 7.08 us -> 8.43 us  [local(): lax.all_to_all(source_spectra.reshape(members, width, 2, bins), 'cross',...]
  transfers between devices with their start and end apart: 4 -> 10, of which waited for: 2 -> 1; matrix products, arithmetic and copies ran while one was open for 6% -> 5% of each run, Pallas kernels for 40% -> 33%
where the time goes in v4:
time: 91.4 us; the launch traced here: 91.1 us
  Pallas kernels  53.7 us (59%)
  starting transfers between devices  23.8 us (26%)
  waiting for transfers between devices  8.46 us (9%)
  other arithmetic  4.61 us (5%)
    pallas_call x4, Pallas kernels, correlate(): pl.pallas_call(functools.partial(correlate_kernel, arrays, int(aliased)),...  48 us
    all_to_all x1, waiting for transfers between devices, local(): lax.all_to_all(source_spectra.reshape(members, width, 2, bins), 'cross',...  8.43 us
    all_to_all x1, starting transfers between devices, local(): lax.all_to_all(source_spectra.reshape(members, width, 2, bins), 'cross',...  8.29 us
    ppermute x1, starting transfers between devices, passed_along(): return lax.ppermute(value, axis, pairs)  5.17 us
    ppermute x3, starting transfers between devices, local(): rest1 = [lax.ppermute(pair1, 'cross', ring) for ring in rings]  4.5 us
    pallas_call x1, Pallas kernels, prepare(): pl.pallas_call(prepare_kernel, out_shape=jax.ShapeDtypeStruct((2, slots,...  4.21 us
    ppermute x3, starting transfers between devices, local(): rest0 = [lax.ppermute(pair0, 'cross', ring) for ring in rings]  2.74 us
    ppermute x1, starting transfers between devices, local(): other1 = lax.ppermute(own[1:], 'cross', across)  2.69 us
  transfers between devices with their start and end apart: 10, of which 1 were waited for; matrix products, arithmetic and copies ran while one was open for 5% of the time, Pallas kernels for 33%

profile of v4, /device:TPU:1, one launch (start us, length us, event | category | flops | bytes accessed | tf_op | source)
XLA Modules:
  0.0 91.1 jit_solution(6625565431093857487)
XLA Ops:
  0.0 8.3 %all-to-all-start = ((f32[8,16,2,1024]{3,2,1,0:T(2,128)}), f32[8,16,2,1024]{3,2,1,0:T(2,128)S(1)}, u32[]{:S(2)}, u32[]{:S(2)}) async-start(f32[8,16,2,1024]{3,2,1,0:T(2,128)} %bitcast.4), calls=%async_computation | async-start | bytes 2097152 | tf_op jit(solution)/shard_map/all_to_all | solution.py:185
  8.3 0.1 broadcast_in_dim.8
  8.4 0.1 sub.17
  8.5 0.1 constant_dynamic-slice_fusion.owners_ref
  8.6 4.2 %prepare.1.refs_1_.refs_3_ = f32[2,128,1024]{2,1,0:T(8,128)} custom-call(s32[1,128]{1,0:T(1,128)} %order_ref.1, s32[128]{0:T(128)} %quality_ref.1, f32[128,2,1024]{2,1,0:T(2,128)} %raw_ref.1), custom_call_target="tpu_custom_call" | custom-call | flops 1310720 | bytes 2097152 | tf_op jit(solution)/shard_map/prepare/pallas_call | solution.py:62
  12.8 2.0 %fusion.6 = bf16[1024,128]{1,0:T(8,128)(2,1)S(1)} fusion(s32[128]{0:T(128)S(1)} %multiply_add_fusion), kind=kLoop, calls=%fused_computation.14 | loop fusion | flops 2621440 | bytes 262656 | tf_op jit(solution)/shard_map/neg | solution.py:188
  14.8 0.0 copy-start.1
  14.8 2.2 %multiply_convert_fusion.1 = (bf16[1024,128]{1,0:T(8,128)(2,1)S(1)}, bf16[1024,128]{1,0:T(8,128)(2,1)S(1)}) fusion(s32[128]{0:T(128)S(1)} %multiply_add_fusion), kind=kLoop, calls=%fused_computation.8 | loop fusion | flops 2490368 | bytes 524800 | tf_op jit(solution)/shard_map/convert_element_type | solution.py:31
  17.1 0.1 maximum_maximum_fusion.refs_2_.refs_4_.refs_5_
  17.2 8.4 %all-to-all-done.shares_ref = f32[8,16,2,1024]{3,2,1,0:T(2,128)S(1)} async-done(((f32[8,16,2,1024]{3,2,1,0:T(2,128)}), f32[8,16,2,1024]{3,2,1,0:T(2,128)S(1)}, u32[]{:S(2)}, u32[]{:S(2)}) %all-to-all-start) | async-done | bytes 1048608 | tf_op jit(solution)/shard_map/all_to_all | solution.py:185
  25.6 1.6 %select.13 = f32[2,16,2,1024]{3,2,1,0:T(2,128)S(1)} custom-call(s32[2,1]{1,0:T(2,128)S(1)} %constant_dynamic-slice_fusion.owners_ref, f32[8,16,2,1024]{3,2,1,0:T(2,128)S(1)} %all-to-all-done.shares_ref), custom_call_target="tpu_custom_call" | custom-call | tf_op jit(solution)/shard_map/select/pallas_call | solution.py:95
  27.2 0.4 collective-permute-start
  27.6 2.7 %collective-permute-start.1 = (f32[1,16,2,1024]{3,2,1,0:T(2,128)S(1)}, f32[1,16,2,1024]{3,2,1,0:T(2,128)S(1)}, u32[]{:S(2)}, u32[]{:S(2)}) collective-permute-start(f32[1,16,2,1024]{3,2,1,0:T(2,128)S(1)} %get-tuple-element.23), channel_id=1, source_target_pairs={{0,4},{1,5},{2,6},{3,7},{4,0},{5,1},{6,2},{7,3},{8,12},{9,13},{10,... | collective-permute-start | bytes 393224 | tf_op jit(solution)/shard_map/ppermute | solution.py:200
  30.3 4.3 %correlate.4.refs_3_ = bf16[2,128,128,256]{3,2,1,0:T(8,128)(2,1)} custom-call(s32[8]{0:T(128)S(1)} %fusion.7.places_ref, f32[1,16,2,1024]{3,2,1,0:T(2,128)S(1)} %get-tuple-element.24.refs_0_, f32[2,128,1024]{2,1,0:T(8,128)S(1)} %copy-done.1, bf16[2048,256]{1,0:T(8,128)(2,1)S(1)} %maximum_maximum_fusion.refs_2_.refs_4_.refs_5_), custom_call_target="tpu_custom_call" | custom-call | flops 2147483648 | bytes 2097152 | tf_op jit(solution)/shard_map/correlate/pallas_call | solution.py:158
  34.6 0.0 collective-permute-done.refs_0_
  34.6 0.1 pad_maximum_fusion.1
  34.7 0.1 collective-permute-start.6
  34.8 2.7 %collective-permute-start.7 = (f32[2,16,2,1024]{3,2,1,0:T(2,128)S(1)}, f32[2,16,2,1024]{3,2,1,0:T(2,128)S(1)}, u32[]{:S(2)}, u32[]{:S(2)}) collective-permute-start(f32[2,16,2,1024]{3,2,1,0:T(2,128)S(1)} %pad_maximum_fusion.1), channel_id=1, source_target_pairs={{0,3},{1,0},{2,1},{3,2},{4,7},{5,4},{6,5},{7,6},{8,11},{9,8},{10,9... | collective-permute-start | bytes 786440 | tf_op jit(solution)/shard_map/ppermute | solution.py:199
  37.5 0.0 collective-permute-start.8
  37.5 0.0 collective-permute-done.1
  37.5 0.1 pad_maximum_fusion.refs_0_
  37.6 4.3 %correlate.5.refs_5_ = bf16[2,128,128,256]{3,2,1,0:T(8,128)(2,1)} custom-call(s32[8]{0:T(128)S(1)} %fusion.7.places_ref, f32[1,16,2,1024]{3,2,1,0:T(2,128)S(1)} %collective-permute-done.refs_0_, f32[2,128,1024]{2,1,0:T(8,128)S(1)} %copy-done.1, bf16[2048,256]{1,0:T(8,128)(2,1)S(1)} %maximum_maximum_fusion.refs_2_.refs_4_.refs_5_, ...), custom_call_target="tpu_custom_call", output_to_operand_aliasing={{}: (4, {})} | custom-call | flops 2147483648 | bytes 2097152 | tf_op jit(solution)/shard_map/correlate/pallas_call | solution.py:158
  41.9 0.6 collective-permute-start.2
  42.5 2.1 %collective-permute-start.3 = (f32[2,16,2,1024]{3,2,1,0:T(2,128)S(1)}, f32[2,16,2,1024]{3,2,1,0:T(2,128)S(1)}, u32[]{:S(2)}, u32[]{:S(2)}) collective-permute-start(f32[2,16,2,1024]{3,2,1,0:T(2,128)S(1)} %pad_maximum_fusion.refs_0_), channel_id=1, source_target_pairs={{0,3},{1,0},{2,1},{3,2},{4,7},{5,4},{6,5},{7,6},{8,11},{9,8},{10,9... | collective-permute-start | bytes 786440 | tf_op jit(solution)/shard_map/ppermute | solution.py:208
  44.6 0.0 collective-permute-done.6.refs_0_
  44.7 1.8 %collective-permute-start.4 = (f32[2,16,2,1024]{3,2,1,0:T(2,128)S(1)}, f32[2,16,2,1024]{3,2,1,0:T(2,128)S(1)}, u32[]{:S(2)}, u32[]{:S(2)}) collective-permute-start(f32[2,16,2,1024]{3,2,1,0:T(2,128)S(1)} %pad_maximum_fusion.refs_0_), channel_id=1, source_target_pairs={{0,2},{1,3},{2,0},{3,1},{4,6},{5,7},{6,4},{7,5},{8,10},{9,11},{10,... | collective-permute-start | bytes 786440 | tf_op jit(solution)/shard_map/ppermute | solution.py:208
  46.4 0.0 collective-permute-done.7.refs_1_
  46.4 5.2 %collective-permute-start.5 = (f32[2,128,1024]{2,1,0:T(8,128)S(1)}, f32[2,128,1024]{2,1,0:T(8,128)S(1)}, u32[]{:S(2)}, u32[]{:S(2)}) collective-permute-start(f32[2,128,1024]{2,1,0:T(8,128)S(1)} %copy-done.1), channel_id=1, source_target_pairs={{0,8},{8,16},{16,24},{24,32},{32,40},{40,48},{48,56},{56,64},{64,7... | collective-permute-start | bytes 3145736 | tf_op jit(solution)/shard_map/ppermute | solution.py:23
  51.6 17.1 %correlate.6.refs_6_ = bf16[2,128,128,256]{3,2,1,0:T(8,128)(2,1)} custom-call(s32[8]{0:T(128)S(1)} %fusion.7.places_ref, f32[2,16,2,1024]{3,2,1,0:T(2,128)S(1)} %collective-permute-done.6.refs_0_, f32[2,16,2,1024]{3,2,1,0:T(2,128)S(1)} %collective-permute-done.7.refs_1_, ...), custom_call_target="tpu_custom_call", output_to_operand_aliasing={{}: (6, {})} | custom-call | flops 12884901888 | bytes 7340032 | tf_op jit(solution)/shard_map/correlate/pallas_call | solution.py:158
  68.7 0.0 collective-permute-done.3.refs_2_
  68.8 0.0 collective-permute-done.4.refs_3_
  68.8 22.2 %correlate.7 = bf16[2,128,128,256]{3,2,1,0:T(8,128)(2,1)} custom-call(s32[8]{0:T(128)S(1)} %fusion.7.places_ref, f32[2,16,2,1024]{3,2,1,0:T(2,128)S(1)} %pad_maximum_fusion.refs_0_, f32[2,16,2,1024]{3,2,1,0:T(2,128)S(1)} %collective-permute-done.2.refs_1_, f32[2,16,2,1024]{3,2,1,0:T(2,128)S(1)} %collective-permute-done.3.refs_2_, ...), custom_call_target="tpu_custom_call", output_to_operand_aliasing={{}: (7, {})} | custom-call | flops 17179869184 | bytes 9437184 | tf_op jit(solution)/shard_map/correlate/pallas_call | solution.py:158
  (12 shorter events, 0.1 us)
Async XLA Ops:
  0.0 8.5 %copy-start = (s32[2,16]{1,0:T(2,128)S(1)}, s32[2,16]{1,0:T(2,128)}, u32[]{:S(2)}) copy-start(s32[2,16]{1,0:T(2,128)} %param.10) | copy-start | bytes 388
  0.0 8.3 %copy-start.2 = (s32[4]{0:T(128)S(1)}, s32[4]{0:T(128)}, u32[]{:S(2)}) copy-start(s32[4]{0:T(128)} %constant.82) | copy-start | bytes 52
  0.0 25.6 %all-to-all-start = ((f32[8,16,2,1024]{3,2,1,0:T(2,128)}), f32[8,16,2,1024]{3,2,1,0:T(2,128)S(1)}, u32[]{:S(2)}, u32[]{:S(2)}) async-start(f32[8,16,2,1024]{3,2,1,0:T(2,128)} %bitcast.4), calls=%async_computation | async-start | bytes 2097152 | tf_op jit(solution)/shard_map/all_to_all | solution.py:185
  14.8 15.4 %copy-start.1 = (f32[2,128,1024]{2,1,0:T(8,128)S(1)}, f32[2,128,1024]{2,1,0:T(8,128)}, u32[]{:S(2)}) copy-start(f32[2,128,1024]{2,1,0:T(8,128)} %prepare.1.refs_1_.refs_3_) | copy-start | bytes 3145732
  27.2 7.4 %collective-permute-start = (f32[1,16,2,1024]{3,2,1,0:T(2,128)S(1)}, f32[1,16,2,1024]{3,2,1,0:T(2,128)S(1)}, u32[]{:S(2)}, u32[]{:S(2)}) collective-permute-start(f32[1,16,2,1024]{3,2,1,0:T(2,128)S(1)} %get-tuple-element.24.refs_0_), channel_id=1, source_target_pairs={{0,4},{1,5},{2,6},{3,7},{4,0},{5,1},{6,2},{7,3},{8,12},{9,13},{10,... | collective-permute-start | bytes 393224 | tf_op jit(solution)/shard_map/ppermute | solution.py:197
  27.6 9.9 %collective-permute-start.1 = (f32[1,16,2,1024]{3,2,1,0:T(2,128)S(1)}, f32[1,16,2,1024]{3,2,1,0:T(2,128)S(1)}, u32[]{:S(2)}, u32[]{:S(2)}) collective-permute-start(f32[1,16,2,1024]{3,2,1,0:T(2,128)S(1)} %get-tuple-element.23), channel_id=1, source_target_pairs={{0,4},{1,5},{2,6},{3,7},{4,0},{5,1},{6,2},{7,3},{8,12},{9,13},{10,... | collective-permute-start | bytes 393224 | tf_op jit(solution)/shard_map/ppermute | solution.py:200
  34.7 9.9 %collective-permute-start.6 = (f32[2,16,2,1024]{3,2,1,0:T(2,128)S(1)}, f32[2,16,2,1024]{3,2,1,0:T(2,128)S(1)}, u32[]{:S(2)}, u32[]{:S(2)}) collective-permute-start(f32[2,16,2,1024]{3,2,1,0:T(2,128)S(1)} %pad_maximum_fusion.1), channel_id=1, source_target_pairs={{0,1},{1,2},{2,3},{3,0},{4,5},{5,6},{6,7},{7,4},{8,9},{9,10},{10,1... | collective-permute-start | bytes 786440 | tf_op jit(solution)/shard_map/ppermute | solution.py:199
  34.8 11.6 %collective-permute-start.7 = (f32[2,16,2,1024]{3,2,1,0:T(2,128)S(1)}, f32[2,16,2,1024]{3,2,1,0:T(2,128)S(1)}, u32[]{:S(2)}, u32[]{:S(2)}) collective-permute-start(f32[2,16,2,1024]{3,2,1,0:T(2,128)S(1)} %pad_maximum_fusion.1), channel_id=1, source_target_pairs={{0,3},{1,0},{2,1},{3,2},{4,7},{5,4},{6,5},{7,6},{8,11},{9,8},{10,9... | collective-permute-start | bytes 786440 | tf_op jit(solution)/shard_map/ppermute | solution.py:199
  37.5 14.1 %collective-permute-start.8 = (f32[2,16,2,1024]{3,2,1,0:T(2,128)S(1)}, f32[2,16,2,1024]{3,2,1,0:T(2,128)S(1)}, u32[]{:S(2)}, u32[]{:S(2)}) collective-permute-start(f32[2,16,2,1024]{3,2,1,0:T(2,128)S(1)} %pad_maximum_fusion.1), channel_id=1, source_target_pairs={{0,2},{1,3},{2,0},{3,1},{4,6},{5,7},{6,4},{7,5},{8,10},{9,11},{10,... | collective-permute-start | bytes 786440 | tf_op jit(solution)/shard_map/ppermute | solution.py:199
  41.9 26.8 %collective-permute-start.2 = (f32[2,16,2,1024]{3,2,1,0:T(2,128)S(1)}, f32[2,16,2,1024]{3,2,1,0:T(2,128)S(1)}, u32[]{:S(2)}, u32[]{:S(2)}) collective-permute-start(f32[2,16,2,1024]{3,2,1,0:T(2,128)S(1)} %pad_maximum_fusion.refs_0_), channel_id=1, source_target_pairs={{0,1},{1,2},{2,3},{3,0},{4,5},{5,6},{6,7},{7,4},{8,9},{9,10},{10,1... | collective-permute-start | bytes 786440 | tf_op jit(solution)/shard_map/ppermute | solution.py:208
  42.5 26.2 %collective-permute-start.3 = (f32[2,16,2,1024]{3,2,1,0:T(2,128)S(1)}, f32[2,16,2,1024]{3,2,1,0:T(2,128)S(1)}, u32[]{:S(2)}, u32[]{:S(2)}) collective-permute-start(f32[2,16,2,1024]{3,2,1,0:T(2,128)S(1)} %pad_maximum_fusion.refs_0_), channel_id=1, source_target_pairs={{0,3},{1,0},{2,1},{3,2},{4,7},{5,4},{6,5},{7,6},{8,11},{9,8},{10,9... | collective-permute-start | bytes 786440 | tf_op jit(solution)/shard_map/ppermute | solution.py:208
  44.7 24.1 %collective-permute-start.4 = (f32[2,16,2,1024]{3,2,1,0:T(2,128)S(1)}, f32[2,16,2,1024]{3,2,1,0:T(2,128)S(1)}, u32[]{:S(2)}, u32[]{:S(2)}) collective-permute-start(f32[2,16,2,1024]{3,2,1,0:T(2,128)S(1)} %pad_maximum_fusion.refs_0_), channel_id=1, source_target_pairs={{0,2},{1,3},{2,0},{3,1},{4,6},{5,7},{6,4},{7,5},{8,10},{9,11},{10,... | collective-permute-start | bytes 786440 | tf_op jit(solution)/shard_map/ppermute | solution.py:208
  46.4 22.4 %collective-permute-start.5 = (f32[2,128,1024]{2,1,0:T(8,128)S(1)}, f32[2,128,1024]{2,1,0:T(8,128)S(1)}, u32[]{:S(2)}, u32[]{:S(2)}) collective-permute-start(f32[2,128,1024]{2,1,0:T(8,128)S(1)} %copy-done.1), channel_id=1, source_target_pairs={{0,8},{8,16},{16,24},{24,32},{32,40},{40,48},{48,56},{56,64},{64,7... | collective-permute-start | bytes 3145736 | tf_op jit(solution)/shard_map/ppermute | solution.py:23

commit v5 on v4

--- a/solution.py
+++ b/solution.py
@@ -13,7 +13,7 @@
 F32 = jnp.float32
 BF16 = jnp.bfloat16
 VMEM = pl.BlockSpec(memory_space=pltpu.VMEM)
-VMEM_BYTES = 24 << 20
+VMEM_BYTES = 40 << 20
 SMALL_VMEM_BYTES = 8 << 20
 
 
@@ -108,7 +108,7 @@
     )(owners, shares)
 
 
-def correlate_kernel(arrays, aliased, places_ref, *refs):
+def correlate_kernel(arrays, aliased, together, columns, where_ref, *refs):
     panel_refs, (slab_ref, table_ref) = refs[:arrays], refs[arrays : arrays + 2]
     out_ref, shares_ref, sems = refs[arrays + 2 + aliased :]
     width = shares_ref.shape[1]
@@ -124,40 +124,50 @@
                 pltpu.make_async_copy(panel_ref.at[row], shares_ref.at[slot], sems.at[slot]).start()
                 slot += 1
 
-    share_ref = shares_ref.at[step]
-    pltpu.make_async_copy(panel_refs[0].at[0], share_ref, sems.at[step]).wait()
+    for i in range(together):
+        slot = step * together + i
+        pltpu.make_async_copy(panel_refs[0].at[0], shares_ref.at[slot], sems.at[slot]).wait()
     slab_re, slab_im = slab_ref[0], slab_ref[1]
-    for first in range(0, width, group):
-        rows = []
-        for p in range(first, first + group):
-            pair = share_ref[p]
-            re, im = pair[0:1, :], pair[1:2, :]
-            inphase = (re * slab_re + im * slab_im).astype(BF16)
-            quadrature = (im * slab_re - re * slab_im).astype(BF16)
-            rows.append(jnp.concatenate([inphase, quadrature], axis=1))
-        sums = jnp.dot(jnp.concatenate(rows, axis=0), table_ref[...], preferred_element_type=F32)
-        for p in range(group):
-            out_ref[first + p] = sums[p * slots : (p + 1) * slots].astype(BF16)
-
-
-def correlate(out, step, panels, places, first, slab, table, sources):
+    for i in range(together):
+        share_ref = shares_ref.at[step * together + lax.rem(lax.div(where_ref[0], columns) + i, together)]
+        for first in range(0, width, group):
+            rows = []
+            for p in range(first, first + group):
+                pair = share_ref[p]
+                re, im = pair[0:1, :], pair[1:2, :]
+                inphase = (re * slab_re + im * slab_im).astype(BF16)
+                quadrature = (im * slab_re - re * slab_im).astype(BF16)
+                rows.append(jnp.concatenate([inphase, quadrature], axis=1))
+            sums = jnp.dot(jnp.concatenate(rows, axis=0), table_ref[...], preferred_element_type=F32)
+            for p in range(group):
+                out_ref[i, first + p] = sums[p * slots : (p + 1) * slots].astype(BF16)
+
+
+def correlate(out, step, panels, where, first, slab, table, columns, shifts, half=None):
     width, _, bins = panels[0].shape[1:]
     slots = slab.shape[1]
     lags = table.shape[1]
     arrays = len(panels)
     count = sum(panel.shape[0] for panel in panels)
+    together = 2 if half is None else 1
     aliased = out is not None
     anywhere = pl.BlockSpec(memory_space=pl.ANY)
+
+    def block(i, where):
+        row = 0 if half is None else lax.rem(lax.div(where[0], columns) + half, 2)
+        shift = sum(((i + first == a).astype(jnp.int32) * d for a, d in enumerate(shifts) if d), 0)
+        return (step, row, lax.rem(where[0] + (columns - shift), columns), 0, 0, 0)
+
     grid_spec = pltpu.PrefetchScalarGridSpec(
         num_scalar_prefetch=1,
-        grid=(count,),
+        grid=(count // together,),
         in_specs=[anywhere] * arrays + [VMEM, VMEM] + [anywhere] * aliased,
-        out_specs=pl.BlockSpec((None, width, slots, lags), lambda i, members: (step, members[first + i], 0, 0)),
+        out_specs=pl.BlockSpec((None, together, None, width, slots, lags), block),
         scratch_shapes=[pltpu.VMEM((count, width, 2, bins), F32), pltpu.SemaphoreType.DMA((count,))],
     )
     return pl.pallas_call(
-        functools.partial(correlate_kernel, arrays, int(aliased)),
-        out_shape=jax.ShapeDtypeStruct((STEPS, sources, slots, lags), BF16),
+        functools.partial(correlate_kernel, arrays, int(aliased), together, columns),
+        out_shape=jax.ShapeDtypeStruct((STEPS, 2, columns, width, slots, lags), BF16),
         grid_spec=grid_spec,
         input_output_aliases={arrays + 3: 0} if aliased else {},
         compiler_params=pltpu.CompilerParams(vmem_limit_bytes=VMEM_BYTES),
@@ -167,7 +177,7 @@
             bytes_accessed=count * width * slots * lags * 2 + 8 * slots * bins,
             transcendentals=0,
         ),
-    )(places, *panels, slab, table, *([out] if aliased else []))
+    )(where, *panels, slab, table, *([out] if aliased else []))
 
 
 def local(receiver_spectra, source_spectra, quality, slot_order, owners):
@@ -177,9 +187,7 @@
     row = members // 2
     me = lax.axis_index("cross")
     shifts = [0, 1, row - 1] + list(range(2, row - 1))
-    order = jnp.arange(members, dtype=jnp.int32)
-    shift = jnp.repeat(jnp.asarray(shifts, jnp.int32), 2)
-    places = (me // row + order) % 2 * row + (me % row + row - shift) % row
+    where = me.astype(jnp.int32).reshape(1)
     mine = lax.dynamic_slice_in_dim(owners, lax.axis_index("blk"), 1, 1)
 
     shares = lax.all_to_all(source_spectra.reshape(members, width, 2, bins), "cross", 0, 0)
@@ -188,7 +196,7 @@
         [jnp.concatenate([cos_table, cos_table], axis=1), jnp.concatenate([sin_table, -sin_table], axis=1)], axis=0
     )
     slab0 = prepare(receiver_spectra, quality, slot_order)
-    shares, slab0, table, places, mine = lax.optimization_barrier((shares, slab0, table, places, mine))
+    shares, slab0, table, where, mine = lax.optimization_barrier((shares, slab0, table, where, mine))
 
     own = select(shares, mine)
     across = [(i, (i + row) % members) for i in range(members)]
@@ -202,13 +210,14 @@
     slab1 = passed_along(sent, "blk", 1)
     pair1 = jnp.concatenate([own[1:], other1], axis=0)
 
-    out = correlate(None, 0, [own[:1]], places, 0, slab0, table, sources)
-    out = correlate(out, 0, [other0], places, 1, slab0, table, sources)
+    out = correlate(None, 0, [own[:1]], where, 0, slab0, table, row, shifts, half=0)
+    out = correlate(out, 0, [other0], where, 0, slab0, table, row, shifts, half=1)
     out, pair1 = lax.optimization_barrier((out, pair1))
     rest1 = [lax.ppermute(pair1, "cross", ring) for ring in rings]
-    out = correlate(out, 0, rest0, places, 2, slab0, table, sources)
-    out = correlate(out, 1, [pair1] + rest1, places, 0, slab1, table, sources)
-    return out[:, None, None]
+    out = correlate(out, 0, rest0, where, 1, slab0, table, row, shifts)
+    out = correlate(out, 1, [pair1] + rest1, where, 0, slab1, table, row, shifts)
+    slots, lags = out.shape[-2:]
+    return out.reshape(STEPS, 1, 1, sources, slots, lags)
 
 
 def solution(mesh):

time: 91.4 us -> 89.3 us (0.977)
  Pallas kernels: 53.7 us -> 50.8 us
    pallas_call x4, Pallas kernels: 48 us -> 45 us  [correlate(): pl.pallas_call(functools.partial(correlate_kernel, arrays, int(aliased),...]
  transfers between devices with their start and end apart: 10 -> 10, of which waited for: 1 -> 1; matrix products, arithmetic and copies ran while one was open for 5% -> 5% of each run, Pallas kernels for 33% -> 31%
where the time goes in v5:
time: 89.3 us; the launch traced here: 88.6 us
  Pallas kernels  50.8 us (57%)
  starting transfers between devices  24.2 us (27%)
  waiting for transfers between devices  8.68 us (10%)
  other arithmetic  4.57 us (5%)
    pallas_call x4, Pallas kernels, correlate(): pl.pallas_call(functools.partial(correlate_kernel, arrays, int(aliased),...  45 us
    all_to_all x1, waiting for transfers between devices, local(): lax.all_to_all(source_spectra.reshape(members, width, 2, bins), 'cross',...  8.66 us
    all_to_all x1, starting transfers between devices, local(): lax.all_to_all(source_spectra.reshape(members, width, 2, bins), 'cross',...  8.29 us
    ppermute x1, starting transfers between devices, passed_along(): return lax.ppermute(value, axis, pairs)  5.64 us
    ppermute x3, starting transfers between devices, local(): rest1 = [lax.ppermute(pair1, 'cross', ring) for ring in rings]  4.5 us
    pallas_call x1, Pallas kernels, prepare(): pl.pallas_call(prepare_kernel, out_shape=jax.ShapeDtypeStruct((2, slots,...  4.2 us
    ppermute x3, starting transfers between devices, local(): rest0 = [lax.ppermute(pair0, 'cross', ring) for ring in rings]  2.74 us
    ppermute x1, starting transfers between devices, local(): other1 = lax.ppermute(own[1:], 'cross', across)  2.69 us
  transfers between devices with their start and end apart: 10, of which 1 were waited for; matrix products, arithmetic and copies ran while one was open for 5% of the time, Pallas kernels for 31%

profile of v5, /device:TPU:1, one launch (start us, length us, event | category | flops | bytes accessed | tf_op | source)
XLA Modules:
  0.0 88.6 jit_solution(4381219817380819639)
XLA Ops:
  0.0 8.3 %all-to-all-start = ((f32[8,16,2,1024]{3,2,1,0:T(2,128)}), f32[8,16,2,1024]{3,2,1,0:T(2,128)S(1)}, u32[]{:S(2)}, u32[]{:S(2)}) async-start(f32[8,16,2,1024]{3,2,1,0:T(2,128)} %bitcast.5), calls=%async_computation | async-start | bytes 2097152 | tf_op jit(solution)/shard_map/all_to_all | solution.py:193
  8.3 4.2 %prepare.1.refs_1_.refs_3_ = f32[2,128,1024]{2,1,0:T(8,128)} custom-call(s32[1,128]{1,0:T(1,128)} %order_ref.1, s32[128]{0:T(128)} %quality_ref.1, f32[128,2,1024]{2,1,0:T(2,128)} %raw_ref.1), custom_call_target="tpu_custom_call" | custom-call | flops 1310720 | bytes 2097152 | tf_op jit(solution)/shard_map/prepare/pallas_call | solution.py:62
  12.5 0.1 constant_dynamic-slice_fusion.owners_ref
  12.6 2.0 %fusion.6 = bf16[1024,128]{1,0:T(8,128)(2,1)S(1)} fusion(s32[128]{0:T(128)S(1)} %multiply_add_fusion), kind=kLoop, calls=%fused_computation.14 | loop fusion | flops 2621440 | bytes 262656 | tf_op jit(solution)/shard_map/neg | solution.py:196
  14.6 0.0 copy-start.1
  14.6 2.2 %multiply_convert_fusion.1 = (bf16[1024,128]{1,0:T(8,128)(2,1)S(1)}, bf16[1024,128]{1,0:T(8,128)(2,1)S(1)}) fusion(s32[128]{0:T(128)S(1)} %multiply_add_fusion), kind=kLoop, calls=%fused_computation.8 | loop fusion | flops 2490368 | bytes 524800 | tf_op jit(solution)/shard_map/convert_element_type | solution.py:31
  16.9 0.1 maximum_maximum_fusion.refs_2_.refs_4_.refs_5_
  17.0 8.7 %all-to-all-done.shares_ref = f32[8,16,2,1024]{3,2,1,0:T(2,128)S(1)} async-done(((f32[8,16,2,1024]{3,2,1,0:T(2,128)}), f32[8,16,2,1024]{3,2,1,0:T(2,128)S(1)}, u32[]{:S(2)}, u32[]{:S(2)}) %all-to-all-start) | async-done | bytes 1048608 | tf_op jit(solution)/shard_map/all_to_all | solution.py:193
  25.6 1.6 %select.3 = f32[2,16,2,1024]{3,2,1,0:T(2,128)S(1)} custom-call(s32[2,1]{1,0:T(2,128)S(1)} %constant_dynamic-slice_fusion.owners_ref, f32[8,16,2,1024]{3,2,1,0:T(2,128)S(1)} %all-to-all-done.shares_ref), custom_call_target="tpu_custom_call" | custom-call | tf_op jit(solution)/shard_map/select/pallas_call | solution.py:95
  27.2 0.4 collective-permute-start
  27.6 2.7 %collective-permute-start.1 = (f32[1,16,2,1024]{3,2,1,0:T(2,128)S(1)}, f32[1,16,2,1024]{3,2,1,0:T(2,128)S(1)}, u32[]{:S(2)}, u32[]{:S(2)}) collective-permute-start(f32[1,16,2,1024]{3,2,1,0:T(2,128)S(1)} %get-tuple-element.23), channel_id=1, source_target_pairs={{0,4},{1,5},{2,6},{3,7},{4,0},{5,1},{6,2},{7,3},{8,12},{9,13},{10,... | collective-permute-start | bytes 393224 | tf_op jit(solution)/shard_map/ppermute | solution.py:208
  30.3 3.7 %correlate.4.refs_3_ = bf16[2,2,4,16,128,256]{5,4,3,2,1,0:T(8,128)(2,1)} custom-call(s32[1]{0:T(128)} %bitcast.1.where_ref, f32[1,16,2,1024]{3,2,1,0:T(2,128)S(1)} %get-tuple-element.24.refs_0_, f32[2,128,1024]{2,1,0:T(8,128)S(1)} %copy-done.1, bf16[2048,256]{1,0:T(8,128)(2,1)S(1)} %maximum_maximum_fusion.refs_2_.refs_4_.refs_5_), custom_call_target="tpu_custom_call" | custom-call | flops 2147483648 | bytes 2097152 | tf_op jit(solution)/shard_map/correlate/pallas_call | solution.py:168
  34.0 0.0 collective-permute-done.refs_0_
  34.0 0.1 pad_maximum_fusion.1
  34.1 0.1 collective-permute-start.6
  34.2 2.7 %collective-permute-start.7 = (f32[2,16,2,1024]{3,2,1,0:T(2,128)S(1)}, f32[2,16,2,1024]{3,2,1,0:T(2,128)S(1)}, u32[]{:S(2)}, u32[]{:S(2)}) collective-permute-start(f32[2,16,2,1024]{3,2,1,0:T(2,128)S(1)} %pad_maximum_fusion.1), channel_id=1, source_target_pairs={{0,3},{1,0},{2,1},{3,2},{4,7},{5,4},{6,5},{7,6},{8,11},{9,8},{10,9... | collective-permute-start | bytes 786440 | tf_op jit(solution)/shard_map/ppermute | solution.py:207
  36.8 0.0 collective-permute-start.8
  36.8 0.0 collective-permute-done.1
  36.8 0.1 pad_maximum_fusion.refs_0_
  37.0 3.7 %correlate.5.refs_5_ = bf16[2,2,4,16,128,256]{5,4,3,2,1,0:T(8,128)(2,1)} custom-call(s32[1]{0:T(128)} %bitcast.1.where_ref, f32[1,16,2,1024]{3,2,1,0:T(2,128)S(1)} %collective-permute-done.refs_0_, f32[2,128,1024]{2,1,0:T(8,128)S(1)} %copy-done.1, bf16[2048,256]{1,0:T(8,128)(2,1)S(1)} %maximum_maximum_fusion.refs_2_.refs_4_.refs_5_, ...), custom_call_target="tpu_custom_call", output_to_operand_aliasing={{}: (4, {})} | custom-call | flops 2147483648 | bytes 2097152 | tf_op jit(solution)/shard_map/correlate/pallas_call | solution.py:168
  40.7 0.6 collective-permute-start.2
  41.3 2.1 %collective-permute-start.3 = (f32[2,16,2,1024]{3,2,1,0:T(2,128)S(1)}, f32[2,16,2,1024]{3,2,1,0:T(2,128)S(1)}, u32[]{:S(2)}, u32[]{:S(2)}) collective-permute-start(f32[2,16,2,1024]{3,2,1,0:T(2,128)S(1)} %pad_maximum_fusion.refs_0_), channel_id=1, source_target_pairs={{0,3},{1,0},{2,1},{3,2},{4,7},{5,4},{6,5},{7,6},{8,11},{9,8},{10,9... | collective-permute-start | bytes 786440 | tf_op jit(solution)/shard_map/ppermute | solution.py:216
  43.4 0.0 collective-permute-done.6.refs_0_
  43.4 1.8 %collective-permute-start.4 = (f32[2,16,2,1024]{3,2,1,0:T(2,128)S(1)}, f32[2,16,2,1024]{3,2,1,0:T(2,128)S(1)}, u32[]{:S(2)}, u32[]{:S(2)}) collective-permute-start(f32[2,16,2,1024]{3,2,1,0:T(2,128)S(1)} %pad_maximum_fusion.refs_0_), channel_id=1, source_target_pairs={{0,2},{1,3},{2,0},{3,1},{4,6},{5,7},{6,4},{7,5},{8,10},{9,11},{10,... | collective-permute-start | bytes 786440 | tf_op jit(solution)/shard_map/ppermute | solution.py:216
  45.2 0.0 collective-permute-done.7.refs_1_
  45.2 5.6 %collective-permute-start.5 = (f32[2,128,1024]{2,1,0:T(8,128)S(1)}, f32[2,128,1024]{2,1,0:T(8,128)S(1)}, u32[]{:S(2)}, u32[]{:S(2)}) collective-permute-start(f32[2,128,1024]{2,1,0:T(8,128)S(1)} %copy-done.1), channel_id=1, source_target_pairs={{0,8},{8,16},{16,24},{24,32},{32,40},{40,48},{48,56},{56,64},{64,7... | collective-permute-start | bytes 3145736 | tf_op jit(solution)/shard_map/ppermute | solution.py:23
  50.8 0.0 collective-permute-done.8.refs_2_
  50.8 16.3 %correlate.6.refs_6_ = bf16[2,2,4,16,128,256]{5,4,3,2,1,0:T(8,128)(2,1)} custom-call(s32[1]{0:T(128)} %bitcast.1.where_ref, f32[2,16,2,1024]{3,2,1,0:T(2,128)S(1)} %collective-permute-done.6.refs_0_, f32[2,16,2,1024]{3,2,1,0:T(2,128)S(1)} %collective-permute-done.7.refs_1_, ...), custom_call_target="tpu_custom_call", output_to_operand_aliasing={{}: (6, {})} | custom-call | flops 12884901888 | bytes 7340032 | tf_op jit(solution)/shard_map/correlate/pallas_call | solution.py:168
  67.1 0.0 collective-permute-done.2.refs_1_
  67.1 0.0 collective-permute-done.3.refs_2_
  67.1 0.0 collective-permute-done.4.refs_3_
  67.2 21.3 %correlate.7 = bf16[2,2,4,16,128,256]{5,4,3,2,1,0:T(8,128)(2,1)} custom-call(s32[1]{0:T(128)} %bitcast.1.where_ref, f32[2,16,2,1024]{3,2,1,0:T(2,128)S(1)} %pad_maximum_fusion.refs_0_, f32[2,16,2,1024]{3,2,1,0:T(2,128)S(1)} %collective-permute-done.2.refs_1_, f32[2,16,2,1024]{3,2,1,0:T(2,128)S(1)} %collective-permute-done.3.refs_2_, ...), custom_call_target="tpu_custom_call", output_to_operand_aliasing={{}: (7, {})} | custom-call | flops 17179869184 | bytes 9437184 | tf_op jit(solution)/shard_map/correlate/pallas_call | solution.py:168
  (6 shorter events, 0.0 us)
Async XLA Ops:
  0.0 12.5 %copy-start = (s32[2,16]{1,0:T(2,128)S(1)}, s32[2,16]{1,0:T(2,128)}, u32[]{:S(2)}) copy-start(s32[2,16]{1,0:T(2,128)} %param.9) | copy-start | bytes 388
  0.0 25.6 %all-to-all-start = ((f32[8,16,2,1024]{3,2,1,0:T(2,128)}), f32[8,16,2,1024]{3,2,1,0:T(2,128)S(1)}, u32[]{:S(2)}, u32[]{:S(2)}) async-start(f32[8,16,2,1024]{3,2,1,0:T(2,128)} %bitcast.5), calls=%async_computation | async-start | bytes 2097152 | tf_op jit(solution)/shard_map/all_to_all | solution.py:193
  14.6 15.7 %copy-start.1 = (f32[2,128,1024]{2,1,0:T(8,128)S(1)}, f32[2,128,1024]{2,1,0:T(8,128)}, u32[]{:S(2)}) copy-start(f32[2,128,1024]{2,1,0:T(8,128)} %prepare.1.refs_1_.refs_3_) | copy-start | bytes 3145732
  27.2 6.8 %collective-permute-start = (f32[1,16,2,1024]{3,2,1,0:T(2,128)S(1)}, f32[1,16,2,1024]{3,2,1,0:T(2,128)S(1)}, u32[]{:S(2)}, u32[]{:S(2)}) collective-permute-start(f32[1,16,2,1024]{3,2,1,0:T(2,128)S(1)} %get-tuple-element.24.refs_0_), channel_id=1, source_target_pairs={{0,4},{1,5},{2,6},{3,7},{4,0},{5,1},{6,2},{7,3},{8,12},{9,13},{10,... | collective-permute-start | bytes 393224 | tf_op jit(solution)/shard_map/ppermute | solution.py:205
  27.6 9.3 %collective-permute-start.1 = (f32[1,16,2,1024]{3,2,1,0:T(2,128)S(1)}, f32[1,16,2,1024]{3,2,1,0:T(2,128)S(1)}, u32[]{:S(2)}, u32[]{:S(2)}) collective-permute-start(f32[1,16,2,1024]{3,2,1,0:T(2,128)S(1)} %get-tuple-element.23), channel_id=1, source_target_pairs={{0,4},{1,5},{2,6},{3,7},{4,0},{5,1},{6,2},{7,3},{8,12},{9,13},{10,... | collective-permute-start | bytes 393224 | tf_op jit(solution)/shard_map/ppermute | solution.py:208
  34.1 9.3 %collective-permute-start.6 = (f32[2,16,2,1024]{3,2,1,0:T(2,128)S(1)}, f32[2,16,2,1024]{3,2,1,0:T(2,128)S(1)}, u32[]{:S(2)}, u32[]{:S(2)}) collective-permute-start(f32[2,16,2,1024]{3,2,1,0:T(2,128)S(1)} %pad_maximum_fusion.1), channel_id=1, source_target_pairs={{0,1},{1,2},{2,3},{3,0},{4,5},{5,6},{6,7},{7,4},{8,9},{9,10},{10,1... | collective-permute-start | bytes 786440 | tf_op jit(solution)/shard_map/ppermute | solution.py:207
  34.2 11.0 %collective-permute-start.7 = (f32[2,16,2,1024]{3,2,1,0:T(2,128)S(1)}, f32[2,16,2,1024]{3,2,1,0:T(2,128)S(1)}, u32[]{:S(2)}, u32[]{:S(2)}) collective-permute-start(f32[2,16,2,1024]{3,2,1,0:T(2,128)S(1)} %pad_maximum_fusion.1), channel_id=1, source_target_pairs={{0,3},{1,0},{2,1},{3,2},{4,7},{5,4},{6,5},{7,6},{8,11},{9,8},{10,9... | collective-permute-start | bytes 786440 | tf_op jit(solution)/shard_map/ppermute | solution.py:207
  36.8 14.0 %collective-permute-start.8 = (f32[2,16,2,1024]{3,2,1,0:T(2,128)S(1)}, f32[2,16,2,1024]{3,2,1,0:T(2,128)S(1)}, u32[]{:S(2)}, u32[]{:S(2)}) collective-permute-start(f32[2,16,2,1024]{3,2,1,0:T(2,128)S(1)} %pad_maximum_fusion.1), channel_id=1, source_target_pairs={{0,2},{1,3},{2,0},{3,1},{4,6},{5,7},{6,4},{7,5},{8,10},{9,11},{10,... | collective-permute-start | bytes 786440 | tf_op jit(solution)/shard_map/ppermute | solution.py:207
  40.7 26.4 %collective-permute-start.2 = (f32[2,16,2,1024]{3,2,1,0:T(2,128)S(1)}, f32[2,16,2,1024]{3,2,1,0:T(2,128)S(1)}, u32[]{:S(2)}, u32[]{:S(2)}) collective-permute-start(f32[2,16,2,1024]{3,2,1,0:T(2,128)S(1)} %pad_maximum_fusion.refs_0_), channel_id=1, source_target_pairs={{0,1},{1,2},{2,3},{3,0},{4,5},{5,6},{6,7},{7,4},{8,9},{9,10},{10,1... | collective-permute-start | bytes 786440 | tf_op jit(solution)/shard_map/ppermute | solution.py:216
  41.3 25.8 %collective-permute-start.3 = (f32[2,16,2,1024]{3,2,1,0:T(2,128)S(1)}, f32[2,16,2,1024]{3,2,1,0:T(2,128)S(1)}, u32[]{:S(2)}, u32[]{:S(2)}) collective-permute-start(f32[2,16,2,1024]{3,2,1,0:T(2,128)S(1)} %pad_maximum_fusion.refs_0_), channel_id=1, source_target_pairs={{0,3},{1,0},{2,1},{3,2},{4,7},{5,4},{6,5},{7,6},{8,11},{9,8},{10,9... | collective-permute-start | bytes 786440 | tf_op jit(solution)/shard_map/ppermute | solution.py:216
  43.4 23.7 %collective-permute-start.4 = (f32[2,16,2,1024]{3,2,1,0:T(2,128)S(1)}, f32[2,16,2,1024]{3,2,1,0:T(2,128)S(1)}, u32[]{:S(2)}, u32[]{:S(2)}) collective-permute-start(f32[2,16,2,1024]{3,2,1,0:T(2,128)S(1)} %pad_maximum_fusion.refs_0_), channel_id=1, source_target_pairs={{0,2},{1,3},{2,0},{3,1},{4,6},{5,7},{6,4},{7,5},{8,10},{9,11},{10,... | collective-permute-start | bytes 786440 | tf_op jit(solution)/shard_map/ppermute | solution.py:216
  45.2 21.9 %collective-permute-start.5 = (f32[2,128,1024]{2,1,0:T(8,128)S(1)}, f32[2,128,1024]{2,1,0:T(8,128)S(1)}, u32[]{:S(2)}, u32[]{:S(2)}) collective-permute-start(f32[2,128,1024]{2,1,0:T(8,128)S(1)} %copy-done.1), channel_id=1, source_target_pairs={{0,8},{8,16},{16,24},{24,32},{32,40},{40,48},{48,56},{56,64},{64,7... | collective-permute-start | bytes 3145736 | tf_op jit(solution)/shard_map/ppermute | solution.py:23

commit v6 on v5

--- a/solution.py
+++ b/solution.py
@@ -204,8 +204,9 @@
 
     other0 = lax.ppermute(own[:1], "cross", across)
     pair0 = jnp.concatenate([own[:1], other0], axis=0)
+    pair0, own1 = lax.optimization_barrier((pair0, own[1:]))
     rest0 = [lax.ppermute(pair0, "cross", ring) for ring in rings]
-    other1 = lax.ppermute(own[1:], "cross", across)
+    other1 = lax.ppermute(own1, "cross", across)
     other1, sent = lax.optimization_barrier((other1, slab0))
     slab1 = passed_along(sent, "blk", 1)
     pair1 = jnp.concatenate([own[1:], other1], axis=0)

time: 89.3 us -> 89 us (level)
  waiting for transfers between devices: 8.68 us -> 11.1 us
  starting transfers between devices: 24.2 us -> 22 us
    ppermute x1, starting transfers between devices: 2.69 us -> 0.9 us  [local(): other1 = lax.ppermute(own1, 'cross', across)]
    ppermute x1, waiting for transfers between devices: 0.01 us -> 1.7 us  [local(): other0 = lax.ppermute(own[:1], 'cross', across)]
  transfers between devices with their start and end apart: 10 -> 10, of which waited for: 1 -> 3; matrix products, arithmetic and copies ran while one was open for 5% -> 5% of each run, Pallas kernels for 31% -> 31%
where the time goes in v6:
time: 89 us; the launch traced here: 88.8 us
  Pallas kernels  50.7 us (57%)
  starting transfers between devices  22 us (25%)
  waiting for transfers between devices  11.1 us (12%)
  other arithmetic  4.57 us (5%)
    pallas_call x4, Pallas kernels, correlate(): pl.pallas_call(functools.partial(correlate_kernel, arrays, int(aliased),...  45 us
    all_to_all x1, waiting for transfers between devices, local(): lax.all_to_all(source_spectra.reshape(members, width, 2, bins), 'cross',...  8.66 us
    all_to_all x1, starting transfers between devices, local(): lax.all_to_all(source_spectra.reshape(members, width, 2, bins), 'cross',...  8.29 us
    ppermute x1, starting transfers between devices, passed_along(): return lax.ppermute(value, axis, pairs)  5.19 us
    ppermute x3, starting transfers between devices, local(): rest1 = [lax.ppermute(pair1, 'cross', ring) for ring in rings]  4.39 us
    pallas_call x1, Pallas kernels, prepare(): pl.pallas_call(prepare_kernel, out_shape=jax.ShapeDtypeStruct((2, slots,...  4.2 us
    ppermute x3, starting transfers between devices, local(): rest0 = [lax.ppermute(pair0, 'cross', ring) for ring in rings]  2.85 us
    convert_element_type x1, other arithmetic, lag_tables(): cos_table = (jnp.cos(phase_angle) / bins).astype(BF16)  2.25 us
  transfers between devices with their start and end apart: 10, of which 3 were waited for; matrix products, arithmetic and copies ran while one was open for 5% of the time, Pallas kernels for 31%

profile of v6, /device:TPU:1, one launch (start us, length us, event | category | flops | bytes accessed | tf_op | source)
XLA Modules:
  0.0 88.8 jit_solution(18329535927655651000)
XLA Ops:
  0.0 8.3 %all-to-all-start = ((f32[8,16,2,1024]{3,2,1,0:T(2,128)}), f32[8,16,2,1024]{3,2,1,0:T(2,128)S(1)}, u32[]{:S(2)}, u32[]{:S(2)}) async-start(f32[8,16,2,1024]{3,2,1,0:T(2,128)} %bitcast.5), calls=%async_computation | async-start | bytes 2097152 | tf_op jit(solution)/shard_map/all_to_all | solution.py:193
  8.3 4.2 %prepare.1.refs_1_.refs_3_ = f32[2,128,1024]{2,1,0:T(8,128)} custom-call(s32[1,128]{1,0:T(1,128)} %order_ref.1, s32[128]{0:T(128)} %quality_ref.1, f32[128,2,1024]{2,1,0:T(2,128)} %raw_ref.1), custom_call_target="tpu_custom_call" | custom-call | flops 1310720 | bytes 2097152 | tf_op jit(solution)/shard_map/prepare/pallas_call | solution.py:62
  12.5 0.1 constant_dynamic-slice_fusion.owners_ref
  12.6 2.0 %fusion.6 = bf16[1024,128]{1,0:T(8,128)(2,1)S(1)} fusion(s32[128]{0:T(128)S(1)} %multiply_add_fusion), kind=kLoop, calls=%fused_computation.14 | loop fusion | flops 2621440 | bytes 262656 | tf_op jit(solution)/shard_map/neg | solution.py:196
  14.6 0.0 copy-start.1
  14.6 2.2 %multiply_convert_fusion.1 = (bf16[1024,128]{1,0:T(8,128)(2,1)S(1)}, bf16[1024,128]{1,0:T(8,128)(2,1)S(1)}) fusion(s32[128]{0:T(128)S(1)} %multiply_add_fusion), kind=kLoop, calls=%fused_computation.8 | loop fusion | flops 2490368 | bytes 524800 | tf_op jit(solution)/shard_map/convert_element_type | solution.py:31
  16.9 0.1 maximum_maximum_fusion.refs_2_.refs_4_.refs_5_
  17.0 8.7 %all-to-all-done.shares_ref = f32[8,16,2,1024]{3,2,1,0:T(2,128)S(1)} async-done(((f32[8,16,2,1024]{3,2,1,0:T(2,128)}), f32[8,16,2,1024]{3,2,1,0:T(2,128)S(1)}, u32[]{:S(2)}, u32[]{:S(2)}) %all-to-all-start) | async-done | bytes 1048608 | tf_op jit(solution)/shard_map/all_to_all | solution.py:193
  25.6 1.6 %select.3 = f32[2,16,2,1024]{3,2,1,0:T(2,128)S(1)} custom-call(s32[2,1]{1,0:T(2,128)S(1)} %constant_dynamic-slice_fusion.owners_ref, f32[8,16,2,1024]{3,2,1,0:T(2,128)S(1)} %all-to-all-done.shares_ref), custom_call_target="tpu_custom_call" | custom-call | tf_op jit(solution)/shard_map/select/pallas_call | solution.py:95
  27.2 0.4 collective-permute-start
  27.6 3.7 %correlate.4.refs_3_ = bf16[2,2,4,16,128,256]{5,4,3,2,1,0:T(8,128)(2,1)} custom-call(s32[1]{0:T(128)} %bitcast.1.where_ref, f32[1,16,2,1024]{3,2,1,0:T(2,128)S(1)} %get-tuple-element.28.refs_0_, f32[2,128,1024]{2,1,0:T(8,128)S(1)} %copy-done.1, bf16[2048,256]{1,0:T(8,128)(2,1)S(1)} %maximum_maximum_fusion.refs_2_.refs_4_.refs_5_), custom_call_target="tpu_custom_call" | custom-call | flops 2147483648 | bytes 2097152 | tf_op jit(solution)/shard_map/correlate/pallas_call | solution.py:168
  31.3 1.7 %collective-permute-done.refs_0_ = f32[1,16,2,1024]{3,2,1,0:T(2,128)S(1)} collective-permute-done((f32[1,16,2,1024]{3,2,1,0:T(2,128)S(1)}, f32[1,16,2,1024]{3,2,1,0:T(2,128)S(1)}, u32[]{:S(2)}, u32[]{:S(2)}) %collective-permute-start) | collective-permute-done | bytes 131104 | tf_op jit(solution)/shard_map/ppermute | solution.py:205
  33.0 0.1 pad_maximum_fusion
  33.1 0.1 collective-permute-start.6
  33.2 2.7 %collective-permute-start.7 = (f32[2,16,2,1024]{3,2,1,0:T(2,128)S(1)}, f32[2,16,2,1024]{3,2,1,0:T(2,128)S(1)}, u32[]{:S(2)}, u32[]{:S(2)}) collective-permute-start(f32[2,16,2,1024]{3,2,1,0:T(2,128)S(1)} %pad_maximum_fusion), channel_id=1, source_target_pairs={{0,3},{1,0},{2,1},{3,2},{4,7},{5,4},{6,5},{7,6},{8,11},{9,8},{10,9... | collective-permute-start | bytes 786440 | tf_op jit(solution)/shard_map/ppermute | solution.py:208
  35.8 0.1 collective-permute-start.8
  35.9 0.9 %collective-permute-start.1 = (f32[1,16,2,1024]{3,2,1,0:T(2,128)S(1)}, f32[1,16,2,1024]{3,2,1,0:T(2,128)S(1)}, u32[]{:S(2)}, u32[]{:S(2)}) collective-permute-start(f32[1,16,2,1024]{3,2,1,0:T(2,128)S(1)} %get-tuple-element.21), channel_id=1, source_target_pairs={{0,4},{1,5},{2,6},{3,7},{4,0},{5,1},{6,2},{7,3},{8,12},{9,13},{10,... | collective-permute-start | bytes 393224 | tf_op jit(solution)/shard_map/ppermute | solution.py:209
  36.8 3.7 %correlate.5.refs_5_ = bf16[2,2,4,16,128,256]{5,4,3,2,1,0:T(8,128)(2,1)} custom-call(s32[1]{0:T(128)} %bitcast.1.where_ref, f32[1,16,2,1024]{3,2,1,0:T(2,128)S(1)} %collective-permute-done.refs_0_, f32[2,128,1024]{2,1,0:T(8,128)S(1)} %copy-done.1, bf16[2048,256]{1,0:T(8,128)(2,1)S(1)} %maximum_maximum_fusion.refs_2_.refs_4_.refs_5_, ...), custom_call_target="tpu_custom_call", output_to_operand_aliasing={{}: (4, {})} | custom-call | flops 2147483648 | bytes 2097152 | tf_op jit(solution)/shard_map/correlate/pallas_call | solution.py:168
  40.5 0.7 collective-permute-done.1
  41.3 0.1 pad_maximum_fusion.1.refs_0_
  41.4 0.5 collective-permute-start.2
  41.9 2.2 %collective-permute-start.3 = (f32[2,16,2,1024]{3,2,1,0:T(2,128)S(1)}, f32[2,16,2,1024]{3,2,1,0:T(2,128)S(1)}, u32[]{:S(2)}, u32[]{:S(2)}) collective-permute-start(f32[2,16,2,1024]{3,2,1,0:T(2,128)S(1)} %pad_maximum_fusion.1.refs_0_), channel_id=1, source_target_pairs={{0,3},{1,0},{2,1},{3,2},{4,7},{5,4},{6,5},{7,6},{8,11},{9,8},{10,9... | collective-permute-start | bytes 786440 | tf_op jit(solution)/shard_map/ppermute | solution.py:217
  44.1 0.0 collective-permute-done.6.refs_0_
  44.1 1.6 %collective-permute-start.4 = (f32[2,16,2,1024]{3,2,1,0:T(2,128)S(1)}, f32[2,16,2,1024]{3,2,1,0:T(2,128)S(1)}, u32[]{:S(2)}, u32[]{:S(2)}) collective-permute-start(f32[2,16,2,1024]{3,2,1,0:T(2,128)S(1)} %pad_maximum_fusion.1.refs_0_), channel_id=1, source_target_pairs={{0,2},{1,3},{2,0},{3,1},{4,6},{5,7},{6,4},{7,5},{8,10},{9,11},{10,... | collective-permute-start | bytes 786440 | tf_op jit(solution)/shard_map/ppermute | solution.py:217
  45.8 0.0 collective-permute-done.7.refs_1_
  45.8 5.2 %collective-permute-start.5 = (f32[2,128,1024]{2,1,0:T(8,128)S(1)}, f32[2,128,1024]{2,1,0:T(8,128)S(1)}, u32[]{:S(2)}, u32[]{:S(2)}) collective-permute-start(f32[2,128,1024]{2,1,0:T(8,128)S(1)} %copy-done.1), channel_id=1, source_target_pairs={{0,8},{8,16},{16,24},{24,32},{32,40},{40,48},{48,56},{56,64},{64,7... | collective-permute-start | bytes 3145736 | tf_op jit(solution)/shard_map/ppermute | solution.py:23
  51.0 0.0 collective-permute-done.8.refs_2_
  51.0 16.3 %correlate.6.refs_6_ = bf16[2,2,4,16,128,256]{5,4,3,2,1,0:T(8,128)(2,1)} custom-call(s32[1]{0:T(128)} %bitcast.1.where_ref, f32[2,16,2,1024]{3,2,1,0:T(2,128)S(1)} %collective-permute-done.6.refs_0_, f32[2,16,2,1024]{3,2,1,0:T(2,128)S(1)} %collective-permute-done.7.refs_1_, ...), custom_call_target="tpu_custom_call", output_to_operand_aliasing={{}: (6, {})} | custom-call | flops 12884901888 | bytes 7340032 | tf_op jit(solution)/shard_map/correlate/pallas_call | solution.py:168
  67.2 0.0 collective-permute-done.2.refs_1_
  67.3 0.0 collective-permute-done.3.refs_2_
  67.3 0.0 collective-permute-done.5.refs_4_
  67.3 21.3 %correlate.7 = bf16[2,2,4,16,128,256]{5,4,3,2,1,0:T(8,128)(2,1)} custom-call(s32[1]{0:T(128)} %bitcast.1.where_ref, f32[2,16,2,1024]{3,2,1,0:T(2,128)S(1)} %pad_maximum_fusion.1.refs_0_, f32[2,16,2,1024]{3,2,1,0:T(2,128)S(1)} %collective-permute-done.2.refs_1_, ...), custom_call_target="tpu_custom_call", output_to_operand_aliasing={{}: (7, {})} | custom-call | flops 17179869184 | bytes 9437184 | tf_op jit(solution)/shard_map/correlate/pallas_call | solution.py:168
  (6 shorter events, 0.0 us)
Async XLA Ops:
  0.0 12.5 %copy-start = (s32[2,16]{1,0:T(2,128)S(1)}, s32[2,16]{1,0:T(2,128)}, u32[]{:S(2)}) copy-start(s32[2,16]{1,0:T(2,128)} %param.9) | copy-start | bytes 388
  0.0 25.6 %all-to-all-start = ((f32[8,16,2,1024]{3,2,1,0:T(2,128)}), f32[8,16,2,1024]{3,2,1,0:T(2,128)S(1)}, u32[]{:S(2)}, u32[]{:S(2)}) async-start(f32[8,16,2,1024]{3,2,1,0:T(2,128)} %bitcast.5), calls=%async_computation | async-start | bytes 2097152 | tf_op jit(solution)/shard_map/all_to_all | solution.py:193
  14.6 13.0 %copy-start.1 = (f32[2,128,1024]{2,1,0:T(8,128)S(1)}, f32[2,128,1024]{2,1,0:T(8,128)}, u32[]{:S(2)}) copy-start(f32[2,128,1024]{2,1,0:T(8,128)} %prepare.1.refs_1_.refs_3_) | copy-start | bytes 3145732
  27.2 5.8 %collective-permute-start = (f32[1,16,2,1024]{3,2,1,0:T(2,128)S(1)}, f32[1,16,2,1024]{3,2,1,0:T(2,128)S(1)}, u32[]{:S(2)}, u32[]{:S(2)}) collective-permute-start(f32[1,16,2,1024]{3,2,1,0:T(2,128)S(1)} %get-tuple-element.28.refs_0_), channel_id=1, source_target_pairs={{0,4},{1,5},{2,6},{3,7},{4,0},{5,1},{6,2},{7,3},{8,12},{9,13},{10,... | collective-permute-start | bytes 393224 | tf_op jit(solution)/shard_map/ppermute | solution.py:205
  33.1 11.1 %collective-permute-start.6 = (f32[2,16,2,1024]{3,2,1,0:T(2,128)S(1)}, f32[2,16,2,1024]{3,2,1,0:T(2,128)S(1)}, u32[]{:S(2)}, u32[]{:S(2)}) collective-permute-start(f32[2,16,2,1024]{3,2,1,0:T(2,128)S(1)} %pad_maximum_fusion), channel_id=1, source_target_pairs={{0,1},{1,2},{2,3},{3,0},{4,5},{5,6},{6,7},{7,4},{8,9},{9,10},{10,1... | collective-permute-start | bytes 786440 | tf_op jit(solution)/shard_map/ppermute | solution.py:208
  33.2 12.6 %collective-permute-start.7 = (f32[2,16,2,1024]{3,2,1,0:T(2,128)S(1)}, f32[2,16,2,1024]{3,2,1,0:T(2,128)S(1)}, u32[]{:S(2)}, u32[]{:S(2)}) collective-permute-start(f32[2,16,2,1024]{3,2,1,0:T(2,128)S(1)} %pad_maximum_fusion), channel_id=1, source_target_pairs={{0,3},{1,0},{2,1},{3,2},{4,7},{5,4},{6,5},{7,6},{8,11},{9,8},{10,9... | collective-permute-start | bytes 786440 | tf_op jit(solution)/shard_map/ppermute | solution.py:208
  35.8 15.2 %collective-permute-start.8 = (f32[2,16,2,1024]{3,2,1,0:T(2,128)S(1)}, f32[2,16,2,1024]{3,2,1,0:T(2,128)S(1)}, u32[]{:S(2)}, u32[]{:S(2)}) collective-permute-start(f32[2,16,2,1024]{3,2,1,0:T(2,128)S(1)} %pad_maximum_fusion), channel_id=1, source_target_pairs={{0,2},{1,3},{2,0},{3,1},{4,6},{5,7},{6,4},{7,5},{8,10},{9,11},{10,... | collective-permute-start | bytes 786440 | tf_op jit(solution)/shard_map/ppermute | solution.py:208
  35.9 5.3 %collective-permute-start.1 = (f32[1,16,2,1024]{3,2,1,0:T(2,128)S(1)}, f32[1,16,2,1024]{3,2,1,0:T(2,128)S(1)}, u32[]{:S(2)}, u32[]{:S(2)}) collective-permute-start(f32[1,16,2,1024]{3,2,1,0:T(2,128)S(1)} %get-tuple-element.21), channel_id=1, source_target_pairs={{0,4},{1,5},{2,6},{3,7},{4,0},{5,1},{6,2},{7,3},{8,12},{9,13},{10,... | collective-permute-start | bytes 393224 | tf_op jit(solution)/shard_map/ppermute | solution.py:209
  41.4 25.9 %collective-permute-start.2 = (f32[2,16,2,1024]{3,2,1,0:T(2,128)S(1)}, f32[2,16,2,1024]{3,2,1,0:T(2,128)S(1)}, u32[]{:S(2)}, u32[]{:S(2)}) collective-permute-start(f32[2,16,2,1024]{3,2,1,0:T(2,128)S(1)} %pad_maximum_fusion.1.refs_0_), channel_id=1, source_target_pairs={{0,1},{1,2},{2,3},{3,0},{4,5},{5,6},{6,7},{7,4},{8,9},{9,10},{10,1... | collective-permute-start | bytes 786440 | tf_op jit(solution)/shard_map/ppermute | solution.py:217
  41.9 25.3 %collective-permute-start.3 = (f32[2,16,2,1024]{3,2,1,0:T(2,128)S(1)}, f32[2,16,2,1024]{3,2,1,0:T(2,128)S(1)}, u32[]{:S(2)}, u32[]{:S(2)}) collective-permute-start(f32[2,16,2,1024]{3,2,1,0:T(2,128)S(1)} %pad_maximum_fusion.1.refs_0_), channel_id=1, source_target_pairs={{0,3},{1,0},{2,1},{3,2},{4,7},{5,4},{6,5},{7,6},{8,11},{9,8},{10,9... | collective-permute-start | bytes 786440 | tf_op jit(solution)/shard_map/ppermute | solution.py:217
  44.1 23.1 %collective-permute-start.4 = (f32[2,16,2,1024]{3,2,1,0:T(2,128)S(1)}, f32[2,16,2,1024]{3,2,1,0:T(2,128)S(1)}, u32[]{:S(2)}, u32[]{:S(2)}) collective-permute-start(f32[2,16,2,1024]{3,2,1,0:T(2,128)S(1)} %pad_maximum_fusion.1.refs_0_), channel_id=1, source_target_pairs={{0,2},{1,3},{2,0},{3,1},{4,6},{5,7},{6,4},{7,5},{8,10},{9,11},{10,... | collective-permute-start | bytes 786440 | tf_op jit(solution)/shard_map/ppermute | solution.py:217
  45.8 21.5 %collective-permute-start.5 = (f32[2,128,1024]{2,1,0:T(8,128)S(1)}, f32[2,128,1024]{2,1,0:T(8,128)S(1)}, u32[]{:S(2)}, u32[]{:S(2)}) collective-permute-start(f32[2,128,1024]{2,1,0:T(8,128)S(1)} %copy-done.1), channel_id=1, source_target_pairs={{0,8},{8,16},{16,24},{24,32},{32,40},{40,48},{48,56},{56,64},{64,7... | collective-permute-start | bytes 3145736 | tf_op jit(solution)/shard_map/ppermute | solution.py:23

commit v7 on v6

--- a/solution.py
+++ b/solution.py
@@ -213,7 +213,6 @@
 
     out = correlate(None, 0, [own[:1]], where, 0, slab0, table, row, shifts, half=0)
     out = correlate(out, 0, [other0], where, 0, slab0, table, row, shifts, half=1)
-    out, pair1 = lax.optimization_barrier((out, pair1))
     rest1 = [lax.ppermute(pair1, "cross", ring) for ring in rings]
     out = correlate(out, 0, rest0, where, 1, slab0, table, row, shifts)
     out = correlate(out, 1, [pair1] + rest1, where, 0, slab1, table, row, shifts)

time: 89 us -> 89 us (level)
  no operation moved by 1% of the time
where the time goes in v7:
time: 89 us; the launch traced here: 88.8 us
  Pallas kernels  50.7 us (57%)
  starting transfers between devices  22 us (25%)
  waiting for transfers between devices  11.1 us (12%)
  other arithmetic  4.57 us (5%)
    pallas_call x4, Pallas kernels, correlate(): pl.pallas_call(functools.partial(correlate_kernel, arrays, int(aliased),...  45 us
    all_to_all x1, waiting for transfers between devices, local(): lax.all_to_all(source_spectra.reshape(members, width, 2, bins), 'cross',...  8.66 us
    all_to_all x1, starting transfers between devices, local(): lax.all_to_all(source_spectra.reshape(members, width, 2, bins), 'cross',...  8.29 us
    ppermute x1, starting transfers between devices, passed_along(): return lax.ppermute(value, axis, pairs)  5.19 us
    ppermute x3, starting transfers between devices, local(): rest1 = [lax.ppermute(pair1, 'cross', ring) for ring in rings]  4.39 us
    pallas_call x1, Pallas kernels, prepare(): pl.pallas_call(prepare_kernel, out_shape=jax.ShapeDtypeStruct((2, slots,...  4.2 us
    ppermute x3, starting transfers between devices, local(): rest0 = [lax.ppermute(pair0, 'cross', ring) for ring in rings]  2.85 us
    convert_element_type x1, other arithmetic, lag_tables(): cos_table = (jnp.cos(phase_angle) / bins).astype(BF16)  2.25 us
  transfers between devices with their start and end apart: 10, of which 3 were waited for; matrix products, arithmetic and copies ran while one was open for 5% of the time, Pallas kernels for 31%

profile of v7, /device:TPU:1, one launch (start us, length us, event | category | flops | bytes accessed | tf_op | source)
XLA Modules:
  0.0 88.8 jit_solution(18329535927655651000)
XLA Ops:
  0.0 8.3 %all-to-all-start = ((f32[8,16,2,1024]{3,2,1,0:T(2,128)}), f32[8,16,2,1024]{3,2,1,0:T(2,128)S(1)}, u32[]{:S(2)}, u32[]{:S(2)}) async-start(f32[8,16,2,1024]{3,2,1,0:T(2,128)} %bitcast.5), calls=%async_computation | async-start | bytes 2097152 | tf_op jit(solution)/shard_map/all_to_all | solution.py:193
  8.3 4.2 %prepare.1.refs_1_.refs_3_ = f32[2,128,1024]{2,1,0:T(8,128)} custom-call(s32[1,128]{1,0:T(1,128)} %order_ref.1, s32[128]{0:T(128)} %quality_ref.1, f32[128,2,1024]{2,1,0:T(2,128)} %raw_ref.1), custom_call_target="tpu_custom_call" | custom-call | flops 1310720 | bytes 2097152 | tf_op jit(solution)/shard_map/prepare/pallas_call | solution.py:62
  12.5 0.1 constant_dynamic-slice_fusion.owners_ref
  12.6 2.0 %fusion.6 = bf16[1024,128]{1,0:T(8,128)(2,1)S(1)} fusion(s32[128]{0:T(128)S(1)} %multiply_add_fusion), kind=kLoop, calls=%fused_computation.14 | loop fusion | flops 2621440 | bytes 262656 | tf_op jit(solution)/shard_map/neg | solution.py:196
  14.6 0.0 copy-start.1
  14.6 2.2 %multiply_convert_fusion.1 = (bf16[1024,128]{1,0:T(8,128)(2,1)S(1)}, bf16[1024,128]{1,0:T(8,128)(2,1)S(1)}) fusion(s32[128]{0:T(128)S(1)} %multiply_add_fusion), kind=kLoop, calls=%fused_computation.8 | loop fusion | flops 2490368 | bytes 524800 | tf_op jit(solution)/shard_map/convert_element_type | solution.py:31
  16.9 0.1 maximum_maximum_fusion.refs_2_.refs_4_.refs_5_
  17.0 8.7 %all-to-all-done.shares_ref = f32[8,16,2,1024]{3,2,1,0:T(2,128)S(1)} async-done(((f32[8,16,2,1024]{3,2,1,0:T(2,128)}), f32[8,16,2,1024]{3,2,1,0:T(2,128)S(1)}, u32[]{:S(2)}, u32[]{:S(2)}) %all-to-all-start) | async-done | bytes 1048608 | tf_op jit(solution)/shard_map/all_to_all | solution.py:193
  25.6 1.6 %select.3 = f32[2,16,2,1024]{3,2,1,0:T(2,128)S(1)} custom-call(s32[2,1]{1,0:T(2,128)S(1)} %constant_dynamic-slice_fusion.owners_ref, f32[8,16,2,1024]{3,2,1,0:T(2,128)S(1)} %all-to-all-done.shares_ref), custom_call_target="tpu_custom_call" | custom-call | tf_op jit(solution)/shard_map/select/pallas_call | solution.py:95
  27.2 0.4 collective-permute-start
  27.6 3.7 %correlate.4.refs_3_ = bf16[2,2,4,16,128,256]{5,4,3,2,1,0:T(8,128)(2,1)} custom-call(s32[1]{0:T(128)} %bitcast.1.where_ref, f32[1,16,2,1024]{3,2,1,0:T(2,128)S(1)} %get-tuple-element.24.refs_0_, f32[2,128,1024]{2,1,0:T(8,128)S(1)} %copy-done.1, bf16[2048,256]{1,0:T(8,128)(2,1)S(1)} %maximum_maximum_fusion.refs_2_.refs_4_.refs_5_), custom_call_target="tpu_custom_call" | custom-call | flops 2147483648 | bytes 2097152 | tf_op jit(solution)/shard_map/correlate/pallas_call | solution.py:168
  31.3 1.7 %collective-permute-done.refs_0_ = f32[1,16,2,1024]{3,2,1,0:T(2,128)S(1)} collective-permute-done((f32[1,16,2,1024]{3,2,1,0:T(2,128)S(1)}, f32[1,16,2,1024]{3,2,1,0:T(2,128)S(1)}, u32[]{:S(2)}, u32[]{:S(2)}) %collective-permute-start) | collective-permute-done | bytes 131104 | tf_op jit(solution)/shard_map/ppermute | solution.py:205
  33.0 0.1 pad_maximum_fusion
  33.1 0.1 collective-permute-start.6
  33.2 2.7 %collective-permute-start.7 = (f32[2,16,2,1024]{3,2,1,0:T(2,128)S(1)}, f32[2,16,2,1024]{3,2,1,0:T(2,128)S(1)}, u32[]{:S(2)}, u32[]{:S(2)}) collective-permute-start(f32[2,16,2,1024]{3,2,1,0:T(2,128)S(1)} %pad_maximum_fusion), channel_id=1, source_target_pairs={{0,3},{1,0},{2,1},{3,2},{4,7},{5,4},{6,5},{7,6},{8,11},{9,8},{10,9... | collective-permute-start | bytes 786440 | tf_op jit(solution)/shard_map/ppermute | solution.py:208
  35.8 0.1 collective-permute-start.8
  35.9 0.9 %collective-permute-start.1 = (f32[1,16,2,1024]{3,2,1,0:T(2,128)S(1)}, f32[1,16,2,1024]{3,2,1,0:T(2,128)S(1)}, u32[]{:S(2)}, u32[]{:S(2)}) collective-permute-start(f32[1,16,2,1024]{3,2,1,0:T(2,128)S(1)} %get-tuple-element.17), channel_id=1, source_target_pairs={{0,4},{1,5},{2,6},{3,7},{4,0},{5,1},{6,2},{7,3},{8,12},{9,13},{10,... | collective-permute-start | bytes 393224 | tf_op jit(solution)/shard_map/ppermute | solution.py:209
  36.8 3.7 %correlate.5.refs_5_ = bf16[2,2,4,16,128,256]{5,4,3,2,1,0:T(8,128)(2,1)} custom-call(s32[1]{0:T(128)} %bitcast.1.where_ref, f32[1,16,2,1024]{3,2,1,0:T(2,128)S(1)} %collective-permute-done.refs_0_, f32[2,128,1024]{2,1,0:T(8,128)S(1)} %copy-done.1, bf16[2048,256]{1,0:T(8,128)(2,1)S(1)} %maximum_maximum_fusion.refs_2_.refs_4_.refs_5_, ...), custom_call_target="tpu_custom_call", output_to_operand_aliasing={{}: (4, {})} | custom-call | flops 2147483648 | bytes 2097152 | tf_op jit(solution)/shard_map/correlate/pallas_call | solution.py:168
  40.5 0.7 collective-permute-done.1
  41.3 0.1 pad_maximum_fusion.1.refs_0_
  41.4 0.5 collective-permute-start.2
  41.9 2.2 %collective-permute-start.3 = (f32[2,16,2,1024]{3,2,1,0:T(2,128)S(1)}, f32[2,16,2,1024]{3,2,1,0:T(2,128)S(1)}, u32[]{:S(2)}, u32[]{:S(2)}) collective-permute-start(f32[2,16,2,1024]{3,2,1,0:T(2,128)S(1)} %pad_maximum_fusion.1.refs_0_), channel_id=1, source_target_pairs={{0,3},{1,0},{2,1},{3,2},{4,7},{5,4},{6,5},{7,6},{8,11},{9,8},{10,9... | collective-permute-start | bytes 786440 | tf_op jit(solution)/shard_map/ppermute | solution.py:216
  44.1 0.0 collective-permute-done.6.refs_0_
  44.1 1.6 %collective-permute-start.4 = (f32[2,16,2,1024]{3,2,1,0:T(2,128)S(1)}, f32[2,16,2,1024]{3,2,1,0:T(2,128)S(1)}, u32[]{:S(2)}, u32[]{:S(2)}) collective-permute-start(f32[2,16,2,1024]{3,2,1,0:T(2,128)S(1)} %pad_maximum_fusion.1.refs_0_), channel_id=1, source_target_pairs={{0,2},{1,3},{2,0},{3,1},{4,6},{5,7},{6,4},{7,5},{8,10},{9,11},{10,... | collective-permute-start | bytes 786440 | tf_op jit(solution)/shard_map/ppermute | solution.py:216
  45.8 0.0 collective-permute-done.7.refs_1_
  45.8 5.2 %collective-permute-start.5 = (f32[2,128,1024]{2,1,0:T(8,128)S(1)}, f32[2,128,1024]{2,1,0:T(8,128)S(1)}, u32[]{:S(2)}, u32[]{:S(2)}) collective-permute-start(f32[2,128,1024]{2,1,0:T(8,128)S(1)} %copy-done.1), channel_id=1, source_target_pairs={{0,8},{8,16},{16,24},{24,32},{32,40},{40,48},{48,56},{56,64},{64,7... | collective-permute-start | bytes 3145736 | tf_op jit(solution)/shard_map/ppermute | solution.py:23
  51.0 0.0 collective-permute-done.8.refs_2_
  51.0 16.3 %correlate.6.refs_6_ = bf16[2,2,4,16,128,256]{5,4,3,2,1,0:T(8,128)(2,1)} custom-call(s32[1]{0:T(128)} %bitcast.1.where_ref, f32[2,16,2,1024]{3,2,1,0:T(2,128)S(1)} %collective-permute-done.6.refs_0_, f32[2,16,2,1024]{3,2,1,0:T(2,128)S(1)} %collective-permute-done.7.refs_1_, ...), custom_call_target="tpu_custom_call", output_to_operand_aliasing={{}: (6, {})} | custom-call | flops 12884901888 | bytes 7340032 | tf_op jit(solution)/shard_map/correlate/pallas_call | solution.py:168
  67.2 0.0 collective-permute-done.2.refs_1_
  67.3 0.0 collective-permute-done.3.refs_2_
  67.3 0.0 collective-permute-done.5.refs_4_
  67.3 21.3 %correlate.7 = bf16[2,2,4,16,128,256]{5,4,3,2,1,0:T(8,128)(2,1)} custom-call(s32[1]{0:T(128)} %bitcast.1.where_ref, f32[2,16,2,1024]{3,2,1,0:T(2,128)S(1)} %pad_maximum_fusion.1.refs_0_, f32[2,16,2,1024]{3,2,1,0:T(2,128)S(1)} %collective-permute-done.2.refs_1_, ...), custom_call_target="tpu_custom_call", output_to_operand_aliasing={{}: (7, {})} | custom-call | flops 17179869184 | bytes 9437184 | tf_op jit(solution)/shard_map/correlate/pallas_call | solution.py:168
  (6 shorter events, 0.0 us)
Async XLA Ops:
  0.0 12.5 %copy-start = (s32[2,16]{1,0:T(2,128)S(1)}, s32[2,16]{1,0:T(2,128)}, u32[]{:S(2)}) copy-start(s32[2,16]{1,0:T(2,128)} %param.9) | copy-start | bytes 388
  0.0 25.6 %all-to-all-start = ((f32[8,16,2,1024]{3,2,1,0:T(2,128)}), f32[8,16,2,1024]{3,2,1,0:T(2,128)S(1)}, u32[]{:S(2)}, u32[]{:S(2)}) async-start(f32[8,16,2,1024]{3,2,1,0:T(2,128)} %bitcast.5), calls=%async_computation | async-start | bytes 2097152 | tf_op jit(solution)/shard_map/all_to_all | solution.py:193
  14.6 13.0 %copy-start.1 = (f32[2,128,1024]{2,1,0:T(8,128)S(1)}, f32[2,128,1024]{2,1,0:T(8,128)}, u32[]{:S(2)}) copy-start(f32[2,128,1024]{2,1,0:T(8,128)} %prepare.1.refs_1_.refs_3_) | copy-start | bytes 3145732
  27.2 5.8 %collective-permute-start = (f32[1,16,2,1024]{3,2,1,0:T(2,128)S(1)}, f32[1,16,2,1024]{3,2,1,0:T(2,128)S(1)}, u32[]{:S(2)}, u32[]{:S(2)}) collective-permute-start(f32[1,16,2,1024]{3,2,1,0:T(2,128)S(1)} %get-tuple-element.24.refs_0_), channel_id=1, source_target_pairs={{0,4},{1,5},{2,6},{3,7},{4,0},{5,1},{6,2},{7,3},{8,12},{9,13},{10,... | collective-permute-start | bytes 393224 | tf_op jit(solution)/shard_map/ppermute | solution.py:205
  33.1 11.1 %collective-permute-start.6 = (f32[2,16,2,1024]{3,2,1,0:T(2,128)S(1)}, f32[2,16,2,1024]{3,2,1,0:T(2,128)S(1)}, u32[]{:S(2)}, u32[]{:S(2)}) collective-permute-start(f32[2,16,2,1024]{3,2,1,0:T(2,128)S(1)} %pad_maximum_fusion), channel_id=1, source_target_pairs={{0,1},{1,2},{2,3},{3,0},{4,5},{5,6},{6,7},{7,4},{8,9},{9,10},{10,1... | collective-permute-start | bytes 786440 | tf_op jit(solution)/shard_map/ppermute | solution.py:208
  33.2 12.6 %collective-permute-start.7 = (f32[2,16,2,1024]{3,2,1,0:T(2,128)S(1)}, f32[2,16,2,1024]{3,2,1,0:T(2,128)S(1)}, u32[]{:S(2)}, u32[]{:S(2)}) collective-permute-start(f32[2,16,2,1024]{3,2,1,0:T(2,128)S(1)} %pad_maximum_fusion), channel_id=1, source_target_pairs={{0,3},{1,0},{2,1},{3,2},{4,7},{5,4},{6,5},{7,6},{8,11},{9,8},{10,9... | collective-permute-start | bytes 786440 | tf_op jit(solution)/shard_map/ppermute | solution.py:208
  35.8 15.2 %collective-permute-start.8 = (f32[2,16,2,1024]{3,2,1,0:T(2,128)S(1)}, f32[2,16,2,1024]{3,2,1,0:T(2,128)S(1)}, u32[]{:S(2)}, u32[]{:S(2)}) collective-permute-start(f32[2,16,2,1024]{3,2,1,0:T(2,128)S(1)} %pad_maximum_fusion), channel_id=1, source_target_pairs={{0,2},{1,3},{2,0},{3,1},{4,6},{5,7},{6,4},{7,5},{8,10},{9,11},{10,... | collective-permute-start | bytes 786440 | tf_op jit(solution)/shard_map/ppermute | solution.py:208
  35.9 5.3 %collective-permute-start.1 = (f32[1,16,2,1024]{3,2,1,0:T(2,128)S(1)}, f32[1,16,2,1024]{3,2,1,0:T(2,128)S(1)}, u32[]{:S(2)}, u32[]{:S(2)}) collective-permute-start(f32[1,16,2,1024]{3,2,1,0:T(2,128)S(1)} %get-tuple-element.17), channel_id=1, source_target_pairs={{0,4},{1,5},{2,6},{3,7},{4,0},{5,1},{6,2},{7,3},{8,12},{9,13},{10,... | collective-permute-start | bytes 393224 | tf_op jit(solution)/shard_map/ppermute | solution.py:209
  41.4 25.9 %collective-permute-start.2 = (f32[2,16,2,1024]{3,2,1,0:T(2,128)S(1)}, f32[2,16,2,1024]{3,2,1,0:T(2,128)S(1)}, u32[]{:S(2)}, u32[]{:S(2)}) collective-permute-start(f32[2,16,2,1024]{3,2,1,0:T(2,128)S(1)} %pad_maximum_fusion.1.refs_0_), channel_id=1, source_target_pairs={{0,1},{1,2},{2,3},{3,0},{4,5},{5,6},{6,7},{7,4},{8,9},{9,10},{10,1... | collective-permute-start | bytes 786440 | tf_op jit(solution)/shard_map/ppermute | solution.py:216
  41.9 25.3 %collective-permute-start.3 = (f32[2,16,2,1024]{3,2,1,0:T(2,128)S(1)}, f32[2,16,2,1024]{3,2,1,0:T(2,128)S(1)}, u32[]{:S(2)}, u32[]{:S(2)}) collective-permute-start(f32[2,16,2,1024]{3,2,1,0:T(2,128)S(1)} %pad_maximum_fusion.1.refs_0_), channel_id=1, source_target_pairs={{0,3},{1,0},{2,1},{3,2},{4,7},{5,4},{6,5},{7,6},{8,11},{9,8},{10,9... | collective-permute-start | bytes 786440 | tf_op jit(solution)/shard_map/ppermute | solution.py:216
  44.1 23.1 %collective-permute-start.4 = (f32[2,16,2,1024]{3,2,1,0:T(2,128)S(1)}, f32[2,16,2,1024]{3,2,1,0:T(2,128)S(1)}, u32[]{:S(2)}, u32[]{:S(2)}) collective-permute-start(f32[2,16,2,1024]{3,2,1,0:T(2,128)S(1)} %pad_maximum_fusion.1.refs_0_), channel_id=1, source_target_pairs={{0,2},{1,3},{2,0},{3,1},{4,6},{5,7},{6,4},{7,5},{8,10},{9,11},{10,... | collective-permute-start | bytes 786440 | tf_op jit(solution)/shard_map/ppermute | solution.py:216
  45.8 21.5 %collective-permute-start.5 = (f32[2,128,1024]{2,1,0:T(8,128)S(1)}, f32[2,128,1024]{2,1,0:T(8,128)S(1)}, u32[]{:S(2)}, u32[]{:S(2)}) collective-permute-start(f32[2,128,1024]{2,1,0:T(8,128)S(1)} %copy-done.1), channel_id=1, source_target_pairs={{0,8},{8,16},{16,24},{24,32},{32,40},{40,48},{48,56},{56,64},{64,7... | collective-permute-start | bytes 3145736 | tf_op jit(solution)/shard_map/ppermute | solution.py:23
